TPU v7x, 32 devices: a whole 2x2x4 slice. The times are simulated.
32 devices in a mesh: gx: 8 (over z, y), gy: 4 (over x, core).
Axes of the slice: x: 2, y: 2, z: 4, core: 2. Of those that a mesh axis runs over, the one named last changes fastest.
Arguments:
- efield: float32 [3, 128, 128, 128], P(None, 'gx', 'gy'), may hold values from -6 to 6
- hfield: float32 [3, 128, 128, 128], P(None, 'gx', 'gy'), may hold values from -6 to 6
- polar: float32 [3, 128, 128, 128], P(None, 'gx', 'gy'), may hold values from -6 to 6
- material_map: int32 [128, 128, 128], P('gx', 'gy'), may hold values from 0 to 2
- via_index: int32 [128, 128, 128], P('gx', 'gy'), may hold values from 0 to 7
- fill_fraction: float32 [128, 128, 128], P('gx', 'gy'), may hold values from 0 to 1
- permittivity: float32 [3], replicated, may hold values from 1 to 5
- conductivity: float32 [3], replicated, may hold values from 0 to 2
- debye_strength: float32 [3], replicated, may hold values from 0.5 to 3
- relax_time: float32 [3], replicated, may hold values from 0.5 to 5
- conformal: float32 [8, 3], replicated, may hold values from 0.3 to 1
Outputs:
- efield_out: float32 [3, 128, 128, 128], P(None, 'gx', 'gy')
- hfield_out: float32 [3, 128, 128, 128], P(None, 'gx', 'gy')
- polar_out: float32 [3, 128, 128, 128], P(None, 'gx', 'gy')
Inputs may be any that keep to these rules, and one draw needn't show every extreme that they name: `via_index`: a row of the conformal table.
All inputs are finite; a program needn't handle non-finite values.
Results may differ from a plain program's by a relative error of at most 0.00002.
Values sent between devices are 32-bit elements; how exact they have to be, the bound alone decides.
A program may use at most 64 MiB of HBM per device.

v0:
```python
import jax
import jax.numpy as jnp
from jax import lax
from jax.sharding import PartitionSpec as P

STEPS = 4


time_step = 0.55


def passed_along(value, axis, steps):
    count = lax.axis_size(axis)
    initial, last = (max(0, -steps), min(count, count - steps))
    return lax.ppermute(value, axis, [(source, source + steps) for source in range(initial, last)])


def select(ids, table, count):
    total = jnp.zeros(ids.shape, jnp.float32)
    for entry in range(count):
        total = total + jnp.where(ids == entry, table[entry], jnp.zeros((), table.dtype))
    return total


def coefficients(
    material_map,
    via_index,
    fill_fraction,
    permittivity,
    conductivity,
    debye_strength,
    relax_time,
    conformal,
):
    count = permittivity.shape[0]
    eps = select(material_map, permittivity, count) * (1.0 + fill_fraction)
    loss = select(material_map, conductivity, count) * time_step / (2.0 * eps)
    ca_coef = (1.0 - loss) / (1.0 + loss)
    cb_coef = time_step / (eps * (1.0 + loss))
    cbp_coef = cb_coef / time_step
    relax = select(material_map, relax_time, count)
    kp_coef = (2.0 * relax - time_step) / (2.0 * relax + time_step)
    bp_coef = (
        2.0 * time_step * select(material_map, debye_strength, count) / (2.0 * relax + time_step)
    )
    vias = conformal.shape[0]
    weights = [cb_coef * select(via_index, conformal[:, comp], vias) for comp in range(3)]
    return jnp.stack([ca_coef, cbp_coef, kp_coef, bp_coef] + weights)


def forward(field, axis, plane):
    rest = lax.slice_in_dim(field, 1, field.shape[axis], axis=axis)
    return jnp.concatenate([rest, plane], axis=axis)


def backward(field, axis, plane):
    rest = lax.slice_in_dim(field, 0, field.shape[axis] - 1, axis=axis)
    return jnp.concatenate([plane, rest], axis=axis)


def curl_e(efield, y_next, x_next):
    ex_comp, ey_comp, ez_comp = (efield[0], efield[1], efield[2])
    z_plane = jnp.zeros_like(ex_comp[:, :, :1])
    cx_part = forward(ez_comp, 1, y_next[1]) - ez_comp - (forward(ey_comp, 2, z_plane) - ey_comp)
    cy_part = forward(ex_comp, 2, z_plane) - ex_comp - (forward(ez_comp, 0, x_next[1]) - ez_comp)
    cz_part = forward(ey_comp, 0, x_next[0]) - ey_comp - (forward(ex_comp, 1, y_next[0]) - ex_comp)
    return jnp.stack([cx_part, cy_part, cz_part])


def curl_h(hfield, y_prev, x_prev):
    hx_comp, hy_comp, hz_comp = (hfield[0], hfield[1], hfield[2])
    z_plane = jnp.zeros_like(hx_comp[:, :, :1])
    cx_part = hz_comp - backward(hz_comp, 1, y_prev[1]) - (hy_comp - backward(hy_comp, 2, z_plane))
    cy_part = hx_comp - backward(hx_comp, 2, z_plane) - (hz_comp - backward(hz_comp, 0, x_prev[1]))
    cz_part = (
        hy_comp - backward(hy_comp, 0, x_prev[0]) - (hx_comp - backward(hx_comp, 1, y_prev[0]))
    )
    return jnp.stack([cx_part, cy_part, cz_part])


def shards(
    efield,
    hfield,
    polar,
    material_map,
    via_index,
    fill_fraction,
    permittivity,
    conductivity,
    debye_strength,
    relax_time,
    conformal,
):
    coef = coefficients(
        material_map,
        via_index,
        fill_fraction,
        permittivity,
        conductivity,
        debye_strength,
        relax_time,
        conformal,
    )
    elec, magn, pol = (efield, hfield, polar)
    for step in range(STEPS):
        y_next = passed_along(jnp.stack([elec[0][:, :1], elec[2][:, :1]]), "gy", -1)
        x_next = passed_along(elec[1:3, :1], "gx", -1)
        magn = magn - time_step * curl_e(elec, y_next, x_next)
        y_prev = passed_along(jnp.stack([magn[0][:, -1:], magn[2][:, -1:]]), "gy", 1)
        x_prev = passed_along(magn[1:3, -1:], "gx", 1)
        pol_new = coef[2] * pol + coef[3] * elec
        elec = coef[0] * elec + coef[4:7] * curl_h(magn, y_prev, x_prev) - coef[1] * (pol_new - pol)
        pol = pol_new
    return (elec, magn, pol)


def solution(mesh):
    placed = (
        P(None, "gx", "gy", None),
        P(None, "gx", "gy", None),
        P(None, "gx", "gy", None),
        P("gx", "gy", None),
        P("gx", "gy", None),
        P("gx", "gy", None),
        P(),
        P(),
        P(),
        P(),
        P(),
    )
    return jax.shard_map(
        shards,
        mesh=mesh,
        in_specs=placed,
        out_specs=(P(None, "gx", "gy", None), P(None, "gx", "gy", None), P(None, "gx", "gy", None)),
        check_vma=False,
    )
```

profile of v0, /device:TPU:9, one launch (start us, length us, event | category | flops | bytes accessed | tf_op | source)
XLA Modules:
  0.0 116.4 jit_solution(638047233057309397)
XLA Ops:
  0.6 0.8 slice.653
  1.4 3.2 %collective-permute-start.1 = (f32[2,1,32,128]{3,2,1,0:T(8,128)S(1)}, f32[2,1,32,128]{3,2,1,0:T(8,128)S(1)}, u32[]{:S(2)}, u32[]{:S(2)}) collective-permute-start(f32[2,1,32,128]{3,2,1,0:T(8,128)S(1)} %slice.653), channel_id=1, source_target_pairs={{4,0},{8,4},{12,8},{16,12},{20,16},{24,20},{28,24},{5,1},{9,5},{13... | collective-permute-start | bytes 98312 | tf_op jit(solution)/shard_map/ppermute | solution.py:15
  4.6 1.2 fusion.57
  6.0 2.9 %collective-permute-start = (f32[2,16,1,128]{3,2,1,0:T(1,128)S(1)}, f32[2,16,1,128]{3,2,1,0:T(1,128)S(1)}, u32[]{:S(2)}, u32[]{:S(2)}) collective-permute-start(f32[2,16,1,128]{3,2,1,0:T(1,128)S(1)} %pad_maximum_fusion.1), channel_id=1, source_target_pairs={{1,0},{2,1},{3,2},{5,4},{6,5},{7,6},{9,8},{10,9},{11,10},{13,12},{... | collective-permute-start | bytes 49160 | tf_op jit(solution)/shard_map/ppermute | solution.py:15
  8.8 0.7 fusion.69
  9.5 0.7 fusion.68
  10.4 0.5 copy-done.8
  10.9 0.6 fusion.72
  11.5 0.6 fusion.73
  12.2 0.7 fusion.71
  12.9 0.7 fusion.70
  13.5 9.6 %multiply_bitcast_fusion.2 = (f32[1,16,32,128]{3,2,1,0:T(8,128)S(1)}, pred[16,32,128]{2,1,0:T(8,128)(4,1)S(1)}, pred[16,32,128]{2,1,0:T(8,128)(4,1)S(1)}, pred[1...) fusion(f32[]{:T(128)} %bitcast.13, f32[]{:T(128)} %bitcast.12, ...), kind=kLoop, calls=%fused_computation.120 | loop fusion | flops 2949120 | bytes 2031672 | tf_op jit(solution)/shard_map/stack | solution.py:48
  23.1 5.3 %multiply_bitcast_fusion = f32[1,16,32,128]{3,2,1,0:T(8,128)S(1)} fusion(f32[16,32,128]{2,1,0:T(8,128)S(1)} %get-tuple-element.14, pred[16,32,128]{2,1,0:T(8,128)(4,1)S(1)} %get-tuple-element.13, pred[16,32,128]{2,1,0:T(8,128)(4,1)S(1)} %get-tuple-element.12, pred[16,32,128]{2,1,0:T(8,128)(4,1)S(1)} %get-tuple-element.11, ...), kind=kLoop, calls=%fused_computation.118 | loop fusion | flops 1048576 | bytes 1048608 | tf_op jit(solution)/shard_map/stack | solution.py:48
  28.4 5.2 %multiply_bitcast_fusion.1 = (f32[1,16,32,128]{3,2,1,0:T(8,128)S(1)}, f32[16,32,128]{2,1,0:T(8,128)S(1)}) fusion(f32[16,32,128]{2,1,0:T(8,128)S(1)} %get-tuple-element.14, pred[16,32,128]{2,1,0:T(8,128)(4,1)S(1)} %get-tuple-element.13, pred[16,32,128]{2,1,0:T(8,128)(4,1)S(1)} %get-tuple-element.12, pred[16,32,128]{2,1,0:T(8,128)(4,1)S(1)} %get-tuple-element.11, ...), kind=kLoop, calls=%fused_computation.119 | loop fusion | flops 1114112 | bytes 1310752 | tf_op jit(solution)/shard_map/stack | solution.py:48
  33.6 7.9 %add_divide_fusion = (f32[16,32,128]{2,1,0:T(8,128)S(1)}, f32[16,32,128]{2,1,0:T(8,128)S(1)}, f32[16,32,128]{2,1,0:T(8,128)S(1)}) fusion(pred[16,32,128]{2,1,0:T(8,128)(4,1)S(1)} %get-tuple-element.17, pred[16,32,128]{2,1,0:T(8,128)(4,1)S(1)} %get-tuple-element.16, pred[16,32,128]{2,1,0:T(8,128)(4,1)S(1)} %get-tuple-element.15, f32[]{:T(128)} %bitcast.60, ...), kind=kLoop, calls=%fused_computation.116 | loop fusion | flops 2228224 | bytes 1245232 | tf_op jit(solution)/shard_map/div | solution.py:42
  42.2 0.2 copy_bitcast_fusion.9
  42.5 0.5 fusion.13
  43.4 0.9 copy-done.2
  44.6 3.0 %collective-permute-start.2 = (f32[2,16,1,128]{3,1,2,0:T(8,128)S(1)}, f32[2,16,1,128]{3,1,2,0:T(8,128)S(1)}, u32[]{:S(2)}, u32[]{:S(2)}) collective-permute-start(f32[2,16,1,128]{3,1,2,0:T(8,128)S(1)} %pad_maximum_fusion.2), channel_id=1, source_target_pairs={{0,1},{1,2},{2,3},{4,5},{5,6},{6,7},{8,9},{9,10},{10,11},{12,13},{... | collective-permute-start | bytes 49160 | tf_op jit(solution)/shard_map/ppermute | solution.py:15
  47.6 2.2 %collective-permute-start.3 = (f32[2,1,32,128]{3,2,1,0:T(8,128)S(1)}, f32[2,1,32,128]{3,2,1,0:T(8,128)S(1)}, u32[]{:S(2)}, u32[]{:S(2)}) collective-permute-start(f32[2,1,32,128]{3,2,1,0:T(8,128)S(1)} %slice.803), channel_id=1, source_target_pairs={{0,4},{4,8},{8,12},{12,16},{16,20},{20,24},{24,28},{1,5},{5,9},{9,... | collective-permute-start | bytes 98312 | tf_op jit(solution)/shard_map/ppermute | solution.py:15
  49.9 3.6 %collective-permute-done.3 = f32[2,1,32,128]{3,2,1,0:T(8,128)S(1)} collective-permute-done((f32[2,1,32,128]{3,2,1,0:T(8,128)S(1)}, f32[2,1,32,128]{3,2,1,0:T(8,128)S(1)}, u32[]{:S(2)}, u32[]{:S(2)}) %collective-permute-start.3) | collective-permute-done | bytes 32800 | tf_op jit(solution)/shard_map/ppermute | solution.py:15
  53.7 0.3 fusion.18
  54.0 0.9 copy-done.3
  54.8 0.5 fusion.2
  55.7 2.3 %collective-permute-start.4 = (f32[2,16,1,128]{3,1,2,0:T(8,128)S(1)}, f32[2,16,1,128]{3,1,2,0:T(8,128)S(1)}, u32[]{:S(2)}, u32[]{:S(2)}) collective-permute-start(f32[2,16,1,128]{3,1,2,0:T(8,128)S(1)} %pad_maximum_fusion.3), channel_id=1, source_target_pairs={{1,0},{2,1},{3,2},{5,4},{6,5},{7,6},{9,8},{10,9},{11,10},{13,12},{... | collective-permute-start | bytes 49160 | tf_op jit(solution)/shard_map/ppermute | solution.py:15
  58.1 0.2 pad_subtract_fusion.3
  58.3 1.9 %collective-permute-start.5 = (f32[2,1,32,128]{3,2,1,0:T(8,128)S(1)}, f32[2,1,32,128]{3,2,1,0:T(8,128)S(1)}, u32[]{:S(2)}, u32[]{:S(2)}) collective-permute-start(f32[2,1,32,128]{3,2,1,0:T(8,128)S(1)} %slice.820), channel_id=1, source_target_pairs={{4,0},{8,4},{12,8},{16,12},{20,16},{24,20},{28,24},{5,1},{9,5},{13... | collective-permute-start | bytes 98312 | tf_op jit(solution)/shard_map/ppermute | solution.py:15
  60.2 0.6 collective-permute-done.4
  61.0 2.3 %collective-permute-done.5 = f32[2,1,32,128]{3,2,1,0:T(8,128)S(1)} collective-permute-done((f32[2,1,32,128]{3,2,1,0:T(8,128)S(1)}, f32[2,1,32,128]{3,2,1,0:T(8,128)S(1)}, u32[]{:S(2)}, u32[]{:S(2)}) %collective-permute-start.5) | collective-permute-done | bytes 32800 | tf_op jit(solution)/shard_map/ppermute | solution.py:15
  63.6 0.2 fusion.23
  63.9 0.3 fusion.3
  64.4 2.6 %collective-permute-start.7 = (f32[2,1,32,128]{3,2,1,0:T(8,128)S(1)}, f32[2,1,32,128]{3,2,1,0:T(8,128)S(1)}, u32[]{:S(2)}, u32[]{:S(2)}) collective-permute-start(f32[2,1,32,128]{3,2,1,0:T(8,128)S(1)} %slice.835), channel_id=1, source_target_pairs={{0,4},{4,8},{8,12},{12,16},{16,20},{20,24},{24,28},{1,5},{5,9},{9,... | collective-permute-start | bytes 98312 | tf_op jit(solution)/shard_map/ppermute | solution.py:15
  67.0 4.4 %collective-permute-start.6 = (f32[2,16,1,128]{3,1,2,0:T(8,128)S(1)}, f32[2,16,1,128]{3,1,2,0:T(8,128)S(1)}, u32[]{:S(2)}, u32[]{:S(2)}) collective-permute-start(f32[2,16,1,128]{3,1,2,0:T(8,128)S(1)} %pad_maximum_fusion.4), channel_id=1, source_target_pairs={{0,1},{1,2},{2,3},{4,5},{5,6},{6,7},{8,9},{9,10},{10,11},{12,13},{... | collective-permute-start | bytes 49160 | tf_op jit(solution)/shard_map/ppermute | solution.py:15
  71.5 0.2 pad_subtract_fusion.2
  71.7 0.6 collective-permute-done.6
  72.5 0.2 slice_bitcast_fusion.19
  72.7 0.2 fusion.28
  72.9 0.6 fusion.5
  73.9 1.9 %collective-permute-start.8 = (f32[2,16,1,128]{3,1,2,0:T(8,128)S(1)}, f32[2,16,1,128]{3,1,2,0:T(8,128)S(1)}, u32[]{:S(2)}, u32[]{:S(2)}) collective-permute-start(f32[2,16,1,128]{3,1,2,0:T(8,128)S(1)} %pad_maximum_fusion.5), channel_id=1, source_target_pairs={{1,0},{2,1},{3,2},{5,4},{6,5},{7,6},{9,8},{10,9},{11,10},{13,12},{... | collective-permute-start | bytes 49160 | tf_op jit(solution)/shard_map/ppermute | solution.py:15
  75.8 0.2 pad_subtract_fusion.1
  76.1 3.5 %collective-permute-start.9 = (f32[2,1,32,128]{3,2,1,0:T(8,128)S(1)}, f32[2,1,32,128]{3,2,1,0:T(8,128)S(1)}, u32[]{:S(2)}, u32[]{:S(2)}) collective-permute-start(f32[2,1,32,128]{3,2,1,0:T(8,128)S(1)} %slice.852), channel_id=1, source_target_pairs={{4,0},{8,4},{12,8},{16,12},{20,16},{24,20},{28,24},{5,1},{9,5},{13... | collective-permute-start | bytes 98312 | tf_op jit(solution)/shard_map/ppermute | solution.py:15
  79.6 0.2 collective-permute-done.8
  80.0 1.1 collective-permute-done.9
  81.3 0.2 fusion.33
  81.6 0.4 fusion.6
  82.2 4.3 %collective-permute-start.11 = (f32[2,1,32,128]{3,2,1,0:T(8,128)S(1)}, f32[2,1,32,128]{3,2,1,0:T(8,128)S(1)}, u32[]{:S(2)}, u32[]{:S(2)}) collective-permute-start(f32[2,1,32,128]{3,2,1,0:T(8,128)S(1)} %slice.867), channel_id=1, source_target_pairs={{0,4},{4,8},{8,12},{12,16},{16,20},{20,24},{24,28},{1,5},{5,9},{9,... | collective-permute-start | bytes 98312 | tf_op jit(solution)/shard_map/ppermute | solution.py:15
  86.5 5.8 %collective-permute-start.10 = (f32[2,16,1,128]{3,1,2,0:T(8,128)S(1)}, f32[2,16,1,128]{3,1,2,0:T(8,128)S(1)}, u32[]{:S(2)}, u32[]{:S(2)}) collective-permute-start(f32[2,16,1,128]{3,1,2,0:T(8,128)S(1)} %pad_maximum_fusion.6), channel_id=1, source_target_pairs={{0,1},{1,2},{2,3},{4,5},{5,6},{6,7},{8,9},{9,10},{10,11},{12,13},{... | collective-permute-start | bytes 49160 | tf_op jit(solution)/shard_map/ppermute | solution.py:15
  92.3 0.2 pad_subtract_fusion
  92.5 0.4 collective-permute-done.10
  93.0 0.2 maximum_subtract_fusion.23
  93.3 0.2 fusion.38
  93.5 0.7 fusion.8
  94.6 1.9 %collective-permute-start.12 = (f32[2,16,1,128]{3,2,1,0:T(1,128)S(1)}, f32[2,16,1,128]{3,2,1,0:T(1,128)S(1)}, u32[]{:S(2)}, u32[]{:S(2)}) collective-permute-start(f32[2,16,1,128]{3,2,1,0:T(1,128)S(1)} %pad_maximum_fusion.7), channel_id=1, source_target_pairs={{1,0},{2,1},{3,2},{5,4},{6,5},{7,6},{9,8},{10,9},{11,10},{13,12},{... | collective-permute-start | bytes 49160 | tf_op jit(solution)/shard_map/ppermute | solution.py:15
  96.7 1.9 %collective-permute-start.13 = (f32[2,1,32,128]{3,2,1,0:T(8,128)S(1)}, f32[2,1,32,128]{3,2,1,0:T(8,128)S(1)}, u32[]{:S(2)}, u32[]{:S(2)}) collective-permute-start(f32[2,1,32,128]{3,2,1,0:T(8,128)S(1)} %slice.884), channel_id=1, source_target_pairs={{4,0},{8,4},{12,8},{16,12},{20,16},{24,20},{28,24},{5,1},{9,5},{13... | collective-permute-start | bytes 98312 | tf_op jit(solution)/shard_map/ppermute | solution.py:15
  99.1 1.1 collective-permute-done.12
  100.2 1.2 %collective-permute-done.13 = f32[2,1,32,128]{3,2,1,0:T(8,128)S(1)} collective-permute-done((f32[2,1,32,128]{3,2,1,0:T(8,128)S(1)}, f32[2,1,32,128]{3,2,1,0:T(8,128)S(1)}, u32[]{:S(2)}, u32[]{:S(2)}) %collective-permute-start.13) | collective-permute-done | bytes 32800 | tf_op jit(solution)/shard_map/ppermute | solution.py:15
  101.4 0.2 copy_bitcast_fusion.4
  101.7 0.5 fusion.43
  102.5 0.5 fusion.9
  103.1 5.4 %collective-permute-start.14 = (f32[2,16,1,128]{3,1,2,0:T(8,128)S(1)}, f32[2,16,1,128]{3,1,2,0:T(8,128)S(1)}, u32[]{:S(2)}, u32[]{:S(2)}) collective-permute-start(f32[2,16,1,128]{3,1,2,0:T(8,128)S(1)} %pad_maximum_fusion.8), channel_id=1, source_target_pairs={{0,1},{1,2},{2,3},{4,5},{5,6},{6,7},{8,9},{9,10},{10,11},{12,13},{... | collective-permute-start | bytes 49160 | tf_op jit(solution)/shard_map/ppermute | solution.py:15
  108.6 2.8 %collective-permute-start.15 = (f32[2,1,32,128]{3,2,1,0:T(8,128)S(1)}, f32[2,1,32,128]{3,2,1,0:T(8,128)S(1)}, u32[]{:S(2)}, u32[]{:S(2)}) collective-permute-start(f32[2,1,32,128]{3,2,1,0:T(8,128)S(1)} %slice.899), channel_id=1, source_target_pairs={{0,4},{4,8},{8,12},{12,16},{16,20},{20,24},{24,28},{1,5},{5,9},{9,... | collective-permute-start | bytes 98312 | tf_op jit(solution)/shard_map/ppermute | solution.py:15
  111.4 2.7 %collective-permute-done.15 = f32[2,1,32,128]{3,2,1,0:T(8,128)S(1)} collective-permute-done((f32[2,1,32,128]{3,2,1,0:T(8,128)S(1)}, f32[2,1,32,128]{3,2,1,0:T(8,128)S(1)}, u32[]{:S(2)}, u32[]{:S(2)}) %collective-permute-start.15) | collective-permute-done | bytes 32800 | tf_op jit(solution)/shard_map/ppermute | solution.py:15
  114.2 0.2 fusion.48
  114.5 2.0 %fusion.11 = (f32[3,16,32,128]{3,2,1,0:T(8,128)}, f32[3,16,32,128]{3,2,1,0:T(8,128)}) fusion(f32[1,16,32,128]{3,2,1,0:T(8,128)S(1)} %get-tuple-element.21, f32[1,16,32,128]{3,2,1,0:T(8,128)S(1)} %get-tuple-element.19, f32[1,16,32,128]{3,2,1,0:T(8,128)S(1)} %get-tuple-element.18, f32[3,16,32,128]{3,2,1,0:T(8,128)S(1)} %fusion.8, ...), kind=kLoop, calls=%fused_computation.20 | loop fusion | flops 4325376 | bytes 8126464 | tf_op jit(solution)/shard_map/sub | solution.py:112
  (138 shorter events, 5.9 us)
Async XLA Ops:
  1.4 8.8 %copy-start = (f32[3,16,32,128]{3,2,1,0:T(8,128)S(1)}, f32[3,16,32,128]{3,2,1,0:T(8,128)}, u32[]{:S(2)}) copy-start(f32[3,16,32,128]{3,2,1,0:T(8,128)} %param.11) | copy-start | bytes 2359300
  1.4 40.8 %collective-permute-start.1 = (f32[2,1,32,128]{3,2,1,0:T(8,128)S(1)}, f32[2,1,32,128]{3,2,1,0:T(8,128)S(1)}, u32[]{:S(2)}, u32[]{:S(2)}) collective-permute-start(f32[2,1,32,128]{3,2,1,0:T(8,128)S(1)} %slice.653), channel_id=1, source_target_pairs={{4,0},{8,4},{12,8},{16,12},{20,16},{24,20},{28,24},{5,1},{9,5},{13... | collective-permute-start | bytes 98312 | tf_op jit(solution)/shard_map/ppermute | solution.py:15
  5.9 2.9 %copy-start.7 = (f32[8,3]{0,1:T(4,128)S(1)}, f32[8,3]{0,1:T(4,128)}, u32[]{:S(2)}) copy-start(f32[8,3]{0,1:T(4,128)} %param.21) | copy-start | bytes 292
  6.0 36.2 %collective-permute-start = (f32[2,16,1,128]{3,2,1,0:T(1,128)S(1)}, f32[2,16,1,128]{3,2,1,0:T(1,128)S(1)}, u32[]{:S(2)}, u32[]{:S(2)}) collective-permute-start(f32[2,16,1,128]{3,2,1,0:T(1,128)S(1)} %pad_maximum_fusion.1), channel_id=1, source_target_pairs={{1,0},{2,1},{3,2},{5,4},{6,5},{7,6},{9,8},{10,9},{11,10},{13,12},{... | collective-permute-start | bytes 49160 | tf_op jit(solution)/shard_map/ppermute | solution.py:15
  10.2 0.7 copy-start.8
  10.3 1.3 %copy-start.9 = (f32[3]{0:T(128)S(1)}, f32[3]{0:T(128)}, u32[]{:S(2)}) copy-start(f32[3]{0:T(128)} %param.18) | copy-start | bytes 40
  10.3 1.9 %copy-start.10 = (f32[3]{0:T(128)S(1)}, f32[3]{0:T(128)}, u32[]{:S(2)}) copy-start(f32[3]{0:T(128)} %param.19) | copy-start | bytes 40
  10.3 2.6 %copy-start.11 = (f32[3]{0:T(128)S(1)}, f32[3]{0:T(128)}, u32[]{:S(2)}) copy-start(f32[3]{0:T(128)} %param.20) | copy-start | bytes 40
  10.3 3.2 %copy-start.4 = (f32[16,32,128]{2,1,0:T(8,128)S(1)}, f32[16,32,128]{2,1,0:T(8,128)}, u32[]{:S(2)}) copy-start(f32[16,32,128]{2,1,0:T(8,128)} %param.16) | copy-start | bytes 786436
  10.3 3.2 %copy-start.5 = (s32[16,32,128]{2,1,0:T(8,128)S(1)}, s32[16,32,128]{2,1,0:T(8,128)}, u32[]{:S(2)}) copy-start(s32[16,32,128]{2,1,0:T(8,128)} %param.15) | copy-start | bytes 786436
  10.3 3.2 %copy-start.6 = (s32[16,32,128]{2,1,0:T(8,128)S(1)}, s32[16,32,128]{2,1,0:T(8,128)}, u32[]{:S(2)}) copy-start(s32[16,32,128]{2,1,0:T(8,128)} %param.14) | copy-start | bytes 786436
  43.1 1.1 copy-start.2
  44.6 5.3 %collective-permute-start.2 = (f32[2,16,1,128]{3,1,2,0:T(8,128)S(1)}, f32[2,16,1,128]{3,1,2,0:T(8,128)S(1)}, u32[]{:S(2)}, u32[]{:S(2)}) collective-permute-start(f32[2,16,1,128]{3,1,2,0:T(8,128)S(1)} %pad_maximum_fusion.2), channel_id=1, source_target_pairs={{0,1},{1,2},{2,3},{4,5},{5,6},{6,7},{8,9},{9,10},{10,11},{12,13},{... | collective-permute-start | bytes 49160 | tf_op jit(solution)/shard_map/ppermute | solution.py:15
  47.6 5.9 %collective-permute-start.3 = (f32[2,1,32,128]{3,2,1,0:T(8,128)S(1)}, f32[2,1,32,128]{3,2,1,0:T(8,128)S(1)}, u32[]{:S(2)}, u32[]{:S(2)}) collective-permute-start(f32[2,1,32,128]{3,2,1,0:T(8,128)S(1)} %slice.803), channel_id=1, source_target_pairs={{0,4},{4,8},{8,12},{12,16},{16,20},{20,24},{24,28},{1,5},{5,9},{9,... | collective-permute-start | bytes 98312 | tf_op jit(solution)/shard_map/ppermute | solution.py:15
  53.7 1.1 copy-start.3
  55.7 5.1 %collective-permute-start.4 = (f32[2,16,1,128]{3,1,2,0:T(8,128)S(1)}, f32[2,16,1,128]{3,1,2,0:T(8,128)S(1)}, u32[]{:S(2)}, u32[]{:S(2)}) collective-permute-start(f32[2,16,1,128]{3,1,2,0:T(8,128)S(1)} %pad_maximum_fusion.3), channel_id=1, source_target_pairs={{1,0},{2,1},{3,2},{5,4},{6,5},{7,6},{9,8},{10,9},{11,10},{13,12},{... | collective-permute-start | bytes 49160 | tf_op jit(solution)/shard_map/ppermute | solution.py:15
  58.3 5.0 %collective-permute-start.5 = (f32[2,1,32,128]{3,2,1,0:T(8,128)S(1)}, f32[2,1,32,128]{3,2,1,0:T(8,128)S(1)}, u32[]{:S(2)}, u32[]{:S(2)}) collective-permute-start(f32[2,1,32,128]{3,2,1,0:T(8,128)S(1)} %slice.820), channel_id=1, source_target_pairs={{4,0},{8,4},{12,8},{16,12},{20,16},{24,20},{28,24},{5,1},{9,5},{13... | collective-permute-start | bytes 98312 | tf_op jit(solution)/shard_map/ppermute | solution.py:15
  64.4 8.1 %collective-permute-start.7 = (f32[2,1,32,128]{3,2,1,0:T(8,128)S(1)}, f32[2,1,32,128]{3,2,1,0:T(8,128)S(1)}, u32[]{:S(2)}, u32[]{:S(2)}) collective-permute-start(f32[2,1,32,128]{3,2,1,0:T(8,128)S(1)} %slice.835), channel_id=1, source_target_pairs={{0,4},{4,8},{8,12},{12,16},{16,20},{20,24},{24,28},{1,5},{5,9},{9,... | collective-permute-start | bytes 98312 | tf_op jit(solution)/shard_map/ppermute | solution.py:15
  67.0 5.3 %collective-permute-start.6 = (f32[2,16,1,128]{3,1,2,0:T(8,128)S(1)}, f32[2,16,1,128]{3,1,2,0:T(8,128)S(1)}, u32[]{:S(2)}, u32[]{:S(2)}) collective-permute-start(f32[2,16,1,128]{3,1,2,0:T(8,128)S(1)} %pad_maximum_fusion.4), channel_id=1, source_target_pairs={{0,1},{1,2},{2,3},{4,5},{5,6},{6,7},{8,9},{9,10},{10,11},{12,13},{... | collective-permute-start | bytes 49160 | tf_op jit(solution)/shard_map/ppermute | solution.py:15
  73.9 5.9 %collective-permute-start.8 = (f32[2,16,1,128]{3,1,2,0:T(8,128)S(1)}, f32[2,16,1,128]{3,1,2,0:T(8,128)S(1)}, u32[]{:S(2)}, u32[]{:S(2)}) collective-permute-start(f32[2,16,1,128]{3,1,2,0:T(8,128)S(1)} %pad_maximum_fusion.5), channel_id=1, source_target_pairs={{1,0},{2,1},{3,2},{5,4},{6,5},{7,6},{9,8},{10,9},{11,10},{13,12},{... | collective-permute-start | bytes 49160 | tf_op jit(solution)/shard_map/ppermute | solution.py:15
  76.1 4.9 %collective-permute-start.9 = (f32[2,1,32,128]{3,2,1,0:T(8,128)S(1)}, f32[2,1,32,128]{3,2,1,0:T(8,128)S(1)}, u32[]{:S(2)}, u32[]{:S(2)}) collective-permute-start(f32[2,1,32,128]{3,2,1,0:T(8,128)S(1)} %slice.852), channel_id=1, source_target_pairs={{4,0},{8,4},{12,8},{16,12},{20,16},{24,20},{28,24},{5,1},{9,5},{13... | collective-permute-start | bytes 98312 | tf_op jit(solution)/shard_map/ppermute | solution.py:15
  82.2 11.0 %collective-permute-start.11 = (f32[2,1,32,128]{3,2,1,0:T(8,128)S(1)}, f32[2,1,32,128]{3,2,1,0:T(8,128)S(1)}, u32[]{:S(2)}, u32[]{:S(2)}) collective-permute-start(f32[2,1,32,128]{3,2,1,0:T(8,128)S(1)} %slice.867), channel_id=1, source_target_pairs={{0,4},{4,8},{8,12},{12,16},{16,20},{20,24},{24,28},{1,5},{5,9},{9,... | collective-permute-start | bytes 98312 | tf_op jit(solution)/shard_map/ppermute | solution.py:15
  86.5 6.5 %collective-permute-start.10 = (f32[2,16,1,128]{3,1,2,0:T(8,128)S(1)}, f32[2,16,1,128]{3,1,2,0:T(8,128)S(1)}, u32[]{:S(2)}, u32[]{:S(2)}) collective-permute-start(f32[2,16,1,128]{3,1,2,0:T(8,128)S(1)} %pad_maximum_fusion.6), channel_id=1, source_target_pairs={{0,1},{1,2},{2,3},{4,5},{5,6},{6,7},{8,9},{9,10},{10,11},{12,13},{... | collective-permute-start | bytes 49160 | tf_op jit(solution)/shard_map/ppermute | solution.py:15
  94.6 5.6 %collective-permute-start.12 = (f32[2,16,1,128]{3,2,1,0:T(1,128)S(1)}, f32[2,16,1,128]{3,2,1,0:T(1,128)S(1)}, u32[]{:S(2)}, u32[]{:S(2)}) collective-permute-start(f32[2,16,1,128]{3,2,1,0:T(1,128)S(1)} %pad_maximum_fusion.7), channel_id=1, source_target_pairs={{1,0},{2,1},{3,2},{5,4},{6,5},{7,6},{9,8},{10,9},{11,10},{13,12},{... | collective-permute-start | bytes 49160 | tf_op jit(solution)/shard_map/ppermute | solution.py:15
  96.7 4.7 %collective-permute-start.13 = (f32[2,1,32,128]{3,2,1,0:T(8,128)S(1)}, f32[2,1,32,128]{3,2,1,0:T(8,128)S(1)}, u32[]{:S(2)}, u32[]{:S(2)}) collective-permute-start(f32[2,1,32,128]{3,2,1,0:T(8,128)S(1)} %slice.884), channel_id=1, source_target_pairs={{4,0},{8,4},{12,8},{16,12},{20,16},{24,20},{28,24},{5,1},{9,5},{13... | collective-permute-start | bytes 98312 | tf_op jit(solution)/shard_map/ppermute | solution.py:15
  103.0 11.2 %copy-start.1 = (f32[3,16,32,128]{3,2,1,0:T(8,128)}, f32[3,16,32,128]{3,2,1,0:T(8,128)S(1)}, u32[]{:S(2)}) copy-start(f32[3,16,32,128]{3,2,1,0:T(8,128)S(1)} %fusion.9) | copy-start | bytes 2359300
  103.1 8.2 %collective-permute-start.14 = (f32[2,16,1,128]{3,1,2,0:T(8,128)S(1)}, f32[2,16,1,128]{3,1,2,0:T(8,128)S(1)}, u32[]{:S(2)}, u32[]{:S(2)}) collective-permute-start(f32[2,16,1,128]{3,1,2,0:T(8,128)S(1)} %pad_maximum_fusion.8), channel_id=1, source_target_pairs={{0,1},{1,2},{2,3},{4,5},{5,6},{6,7},{8,9},{9,10},{10,11},{12,13},{... | collective-permute-start | bytes 49160 | tf_op jit(solution)/shard_map/ppermute | solution.py:15
  108.6 5.6 %collective-permute-start.15 = (f32[2,1,32,128]{3,2,1,0:T(8,128)S(1)}, f32[2,1,32,128]{3,2,1,0:T(8,128)S(1)}, u32[]{:S(2)}, u32[]{:S(2)}) collective-permute-start(f32[2,1,32,128]{3,2,1,0:T(8,128)S(1)} %slice.899), channel_id=1, source_target_pairs={{0,4},{4,8},{8,12},{12,16},{16,20},{20,24},{24,28},{1,5},{5,9},{9,... | collective-permute-start | bytes 98312 | tf_op jit(solution)/shard_map/ppermute | solution.py:15
where the time goes:
time: 118 us; the launch traced here: 116 us
  starting transfers between devices  50 us (42%)
  other arithmetic  38.3 us (32%)
  waiting for transfers between devices  13.8 us (12%)
  local copies, waits for them, and re-layouts  12.5 us (11%)
  between operations  1.79 us (2%)
    ppermute x16, starting transfers between devices, passed_along(): lax.ppermute(value, axis, [(source, source + steps) for source in range(i...  50 us
    another operation x3, other arithmetic, coefficients(): return jnp.stack([ca_coef, cbp_coef, kp_coef, bp_coef] + weights)  20 us
    ppermute x16, waiting for transfers between devices, passed_along(): lax.ppermute(value, axis, [(source, source + steps) for source in range(i...  13.8 us
    div x1, other arithmetic, coefficients(): kp_coef = (2.0 * relax - time_step) / (2.0 * relax + time_step)  7.91 us
    unnamed x38, local copies, waits for them, and re-layouts  4.23 us
    slice x6, local copies, waits for them, and re-layouts, select(): table[entry]  4 us
    sub x4, other arithmetic, shards(): coef[0] * elec + coef[4:7] * curl_h(magn, y_prev, x_prev)  3.81 us
  transfers between devices with their start and end apart: 16, of which 10 were waited for; matrix products, arithmetic and copies ran while one was open for 31% of the time, Pallas kernels for 0%

commit v1 on v0

v1 whole, which is shorter than its diff:
```python
import functools

import jax
import jax.numpy as jnp
from jax import lax
from jax.experimental import pallas as pl
from jax.experimental.pallas import tpu as pltpu
from jax.sharding import PartitionSpec as P

STEPS = 4
DT = 0.55
PAD = 8
MESH = pl.DeviceIdType.MESH


def z_next(value):
    lanes = value.shape[1]
    lane = lax.broadcasted_iota(jnp.int32, value.shape, 1)
    return jnp.where(lane < lanes - 1, pltpu.roll(value, lanes - 1, 1), 0.0)


def z_prev(value):
    lane = lax.broadcasted_iota(jnp.int32, value.shape, 1)
    return jnp.where(lane > 0, pltpu.roll(value, 1, 1), 0.0)


def row_prev(value):
    row = lax.broadcasted_iota(jnp.int32, value.shape, 0)
    return jnp.where(row > 0, pltpu.roll(value, 1, 0), 0.0)


def at_row(line, row, like):
    rows = lax.broadcasted_iota(jnp.int32, like.shape, 0)
    return jnp.where(rows == row, jnp.broadcast_to(line, like.shape), 0.0)


def kernel(
    sizes,
    perm, cond, deb, relax, conf,
    e_in, h_in, p_in, m_in, v_in, f_in,
    e_out, h_out, p_out,
    E, H, Q, M, V, F, C, W,
    sxe, sxa, sye, sya, sce, sca,
    rxe, rxa, rye, rya, rce, rca,
    in_sem, out_sem, send_sem, recv_sem,
):
    count_x, count_y = sizes
    nx, ny, nz = m_in.shape
    mats, vias = perm.shape[0], conf.shape[0]
    gx, gy = lax.axis_index("gx"), lax.axis_index("gy")
    own = pl.ds(PAD, ny)
    last = nx - 1
    end = PAD + ny - 1

    def loads():
        return [
            pltpu.make_async_copy(e_in, E.at[:, 0:nx, 0:ny], in_sem.at[0]),
            pltpu.make_async_copy(h_in, H.at[:, 1 : nx + 1, PAD : PAD + ny], in_sem.at[1]),
            pltpu.make_async_copy(m_in, M, in_sem.at[2]),
            pltpu.make_async_copy(v_in, V, in_sem.at[3]),
            pltpu.make_async_copy(f_in, F, in_sem.at[4]),
            pltpu.make_async_copy(p_in, Q, in_sem.at[5]),
        ]

    low_x, high_x = gx > 0, gx < count_x - 1
    low_y, high_y = gy > 0, gy < count_y - 1
    routes = [
        ((gx - 1, gy), low_x, sxe, rxe, high_x),
        ((gx + 1, gy), high_x, sxa, rxa, low_x),
        ((gx, gy - 1), low_y, sye, rye, high_y),
        ((gx, gy + 1), high_y, sya, rya, low_y),
        ((gx + 1, gy - 1), high_x & low_y, sce, rce, low_x & high_y),
        ((gx - 1, gy + 1), low_x & high_y, sca, rca, high_x & low_y),
    ]

    barrier = pltpu.get_barrier_semaphore()
    for target, there, _, _, _ in routes:
        @pl.when(there)
        def _(target=target):
            pl.semaphore_signal(barrier, inc=1, device_id=target, device_id_type=MESH)

    for copy in loads():
        copy.start()

    def remote(k, t):
        target, _, source, dest, _ = routes[k]
        return pltpu.make_async_remote_copy(
            src_ref=source.at[t],
            dst_ref=dest.at[t],
            send_sem=send_sem.at[k, t],
            recv_sem=recv_sem.at[k, t],
            device_id=target,
            device_id_type=MESH,
        )

    def send(t):
        for k in range(len(routes)):
            @pl.when(routes[k][1])
            def _(k=k):
                remote(k, t).start()

    def wait_sent(t):
        for k in range(len(routes)):
            @pl.when(routes[k][1])
            def _(k=k):
                remote(k, t).wait_send()

    def wait_arrived(t):
        for k in range(len(routes)):
            @pl.when(routes[k][4])
            def _(k=k):
                remote(k, t).wait_recv()

    for _, _, _, dest, sender in routes:
        @pl.when(jnp.logical_not(sender))
        def _(dest=dest):
            dest[...] = jnp.zeros(dest.shape, jnp.float32)

    for comp in range(3):
        E[comp, nx] = jnp.zeros((ny + PAD, nz), jnp.float32)
        H[comp, 0] = jnp.zeros((ny + PAD, nz), jnp.float32)
        for x in range(nx):
            E[comp, x, ny : ny + PAD] = jnp.zeros((PAD, nz), jnp.float32)
            H[comp, x + 1, 0:PAD] = jnp.zeros((PAD, nz), jnp.float32)

    def stage(t):
        sxe[t] = E[1:3, 0, 0:ny]
        ex = E[0, last, 0:ny]
        sxa[t, 0] = H[1, nx, own] - DT * (z_next(ex) - ex + E[2, last, 0:ny])
        sxa[t, 1] = H[2, nx, own] + DT * (E[1, last, 0:ny] + E[0, last, 1 : ny + 1] - ex)
        sce[t] = E[0, last, 0:8]
        sca[t] = E[1, 0, ny - 8 : ny]
        sye[t, 0] = E[0, 0:nx, 0, :]
        sye[t, 1] = E[2, 0:nx, 0, :]
        ey = E[1, 0:nx, ny - 1, :]
        sya[t, 0] = H[0, 1 : nx + 1, end, :] + DT * (E[2, 0:nx, ny - 1, :] + z_next(ey) - ey)
        sya[t, 1] = H[2, 1 : nx + 1, end, :] - DT * (
            E[1, 1 : nx + 1, ny - 1, :] - ey + E[0, 0:nx, ny - 1, :]
        )

    copies = loads()
    copies[0].wait()
    copies[1].wait()
    stage(0)
    pl.semaphore_wait(barrier, sum(jnp.where(route[1], 1, 0) for route in routes))
    send(0)

    for copy in copies[2:5]:
        copy.wait()
    shape = (ny, nz)
    mat_eps = [jnp.full(shape, perm[m], jnp.float32) for m in range(mats)]
    mat_loss = [jnp.full(shape, cond[m] * (0.5 * DT), jnp.float32) for m in range(mats)]
    mat_kp, mat_bp = [], []
    for m in range(mats):
        tau = jnp.full(shape, 2.0 * relax[m], jnp.float32)
        mat_kp.append((tau - DT) / (tau + DT))
        mat_bp.append(jnp.full(shape, 2.0 * DT * deb[m], jnp.float32) / (tau + DT))

    def pick(ids, table):
        value = table[-1]
        for entry in range(len(table) - 2, -1, -1):
            value = jnp.where(ids == entry, table[entry], value)
        return value

    def coefficients(x, carry):
        ids, rows = M[x], V[x]
        eps = pick(ids, mat_eps) * (1.0 + F[x])
        loss = pick(ids, mat_loss)
        kp, bp = pick(ids, mat_kp), pick(ids, mat_bp)
        inv = 1.0 / (eps + loss)
        C[0, x] = (eps - loss - bp) * inv
        C[1, x] = (1.0 - kp) * inv
        C[2, x] = kp
        C[3, x] = bp
        inv = inv * DT
        for comp in range(3):
            C[4 + comp, x] = inv * pick(rows, [conf[row, comp] for row in range(vias)])
        return carry

    lax.fori_loop(0, nx, coefficients, 0, unroll=2)
    for comp in range(3):
        W[comp, 0] = C[4 + comp, :, 0, :]
        W[comp, 1] = C[4 + comp, :, ny - 1, :]
    copies[5].wait()

    flag_x = jnp.where(low_x, 1.0, 0.0)
    flag_y = jnp.where(low_y, 1.0, 0.0)

    def interior(x, carry):
        ex, ey, ez = E[0, x, 0:ny], E[1, x, 0:ny], E[2, x, 0:ny]
        ex_y, ez_y = E[0, x, 1 : ny + 1], E[2, x, 1 : ny + 1]
        ey_x, ez_x = E[1, x + 1, 0:ny], E[2, x + 1, 0:ny]
        hx = H[0, x + 1, own] - DT * ((ez_y - ez) - (z_next(ey) - ey))
        hy = H[1, x + 1, own] - DT * ((z_next(ex) - ex) - (ez_x - ez))
        hz = H[2, x + 1, own] - DT * ((ey_x - ey) - (ex_y - ex))
        H[0, x + 1, own], H[1, x + 1, own], H[2, x + 1, own] = hx, hy, hz
        below = pl.ds(PAD - 1, ny)
        cx = (hz - H[2, x + 1, below]) - (hy - z_prev(hy))
        cy = (hx - z_prev(hx)) - (hz - H[2, x, own])
        cz = (hy - H[1, x, own]) - (hx - H[0, x + 1, below])
        c1, c2, kp, bp = C[0, x], C[1, x], C[2, x], C[3, x]
        for comp, (value, curl) in enumerate(((ex, cx), (ey, cy), (ez, cz))):
            pol = Q[comp, x]
            E[comp, x, 0:ny] = c1 * value + c2 * pol + C[4 + comp, x] * curl
            Q[comp, x] = kp * pol + bp * value
        return carry

    def correct(t):
        dhx, dhz = -DT * rye[t, 1], DT * rye[t, 0]
        H[0, 1 : nx + 1, end, :] += dhx
        H[2, 1 : nx + 1, end, :] += dhz
        E[0, 0:nx, ny - 1, :] += W[0, 1] * dhz
        E[1, 0:nx, ny - 1, :] += W[1, 1] * ((dhx - z_prev(dhx)) - (dhz - row_prev(dhz)))
        E[2, 0:nx, ny - 1, :] -= W[2, 1] * dhx
        hx = flag_y * (rya[t, 0] - DT * sye[t, 1])
        hz = flag_y * (rya[t, 1] + DT * (sye[t, 0] - at_row(rca[t, 7:8], last, dhx)))
        E[0, 0:nx, 0, :] -= W[0, 0] * hz
        E[2, 0:nx, 0, :] += W[2, 0] * hx
        dhy, dhz = DT * rxe[t, 1], -DT * rxe[t, 0]
        H[1, nx, own] += dhy
        H[2, nx, own] += dhz
        E[0, last, 0:ny] += C[4, last] * ((dhz - row_prev(dhz)) - (dhy - z_prev(dhy)))
        E[1, last, 0:ny] -= C[5, last] * dhz
        E[2, last, 0:ny] += C[6, last] * dhy
        hy = flag_x * (rxa[t, 0] + DT * sxe[t, 1])
        hz = flag_x * (rxa[t, 1] - DT * (sxe[t, 0] - at_row(rce[t, 0:1], ny - 1, dhy)))
        E[1, 0, 0:ny] += C[5, 0] * hz
        E[2, 0, 0:ny] -= C[6, 0] * hy

    def advance(t, carry):
        lax.fori_loop(0, nx, interior, 0, unroll=2)
        wait_arrived(t)
        correct(t)

        @pl.when(t < STEPS - 1)
        def _():
            stage(t + 1)
            send(t + 1)

        wait_sent(t)
        return carry

    lax.fori_loop(0, STEPS, advance, 0)

    outs = [
        pltpu.make_async_copy(E.at[:, 0:nx, 0:ny], e_out, out_sem.at[0]),
        pltpu.make_async_copy(H.at[:, 1 : nx + 1, PAD : PAD + ny], h_out, out_sem.at[1]),
        pltpu.make_async_copy(Q, p_out, out_sem.at[2]),
    ]
    for copy in outs:
        copy.start()
    for copy in outs:
        copy.wait()


def shards(sizes, efield, hfield, polar, material_map, via_index, fill, perm, cond, deb, relax, conf):
    nx, ny, nz = material_map.shape
    f32 = jnp.float32
    block = jax.ShapeDtypeStruct(efield.shape, f32)
    planes = [
        pltpu.VMEM((STEPS, 2, ny, nz), f32),
        pltpu.VMEM((STEPS, 2, ny, nz), f32),
        pltpu.VMEM((STEPS, 2, nx, nz), f32),
        pltpu.VMEM((STEPS, 2, nx, nz), f32),
        pltpu.VMEM((STEPS, 8, nz), f32),
        pltpu.VMEM((STEPS, 8, nz), f32),
    ]
    smem = pl.BlockSpec(memory_space=pltpu.SMEM)
    hbm = pl.BlockSpec(memory_space=pl.ANY)
    return pl.pallas_call(
        functools.partial(kernel, sizes),
        out_shape=(block, block, block),
        in_specs=[smem] * 5 + [hbm] * 6,
        out_specs=(hbm, hbm, hbm),
        scratch_shapes=[
            pltpu.VMEM((3, nx + 1, ny + PAD, nz), f32),
            pltpu.VMEM((3, nx + 1, ny + PAD, nz), f32),
            pltpu.VMEM((3, nx, ny, nz), f32),
            pltpu.VMEM((nx, ny, nz), jnp.int32),
            pltpu.VMEM((nx, ny, nz), jnp.int32),
            pltpu.VMEM((nx, ny, nz), f32),
            pltpu.VMEM((7, nx, ny, nz), f32),
            pltpu.VMEM((3, 2, nx, nz), f32),
        ]
        + planes
        + planes
        + [
            pltpu.SemaphoreType.DMA((6,)),
            pltpu.SemaphoreType.DMA((3,)),
            pltpu.SemaphoreType.DMA((6, STEPS)),
            pltpu.SemaphoreType.DMA((6, STEPS)),
        ],
        compiler_params=pltpu.CompilerParams(
            collective_id=0, has_side_effects=True, vmem_limit_bytes=32 * 1024 * 1024
        ),
        cost_estimate=pl.CostEstimate(
            flops=80 * STEPS * nx * ny * nz, bytes_accessed=21 * 4 * nx * ny * nz, transcendentals=0
        ),
        name="yee_steps",
    )(perm, cond, deb, relax, conf, efield, hfield, polar, material_map, via_index, fill)


def solution(mesh):
    field, cell = P(None, "gx", "gy", None), P("gx", "gy", None)
    return jax.shard_map(
        functools.partial(shards, (mesh.shape["gx"], mesh.shape["gy"])),
        mesh=mesh,
        in_specs=(field, field, field, cell, cell, cell, P(), P(), P(), P(), P()),
        out_specs=(field, field, field),
        check_vma=False,
    )
```

time: 118 us -> 30.1 us (0.26)
  the two profiles are of different devices: /device:TPU:9 before, /device:TPU:0 now
where the time goes in v1:
time: 30.1 us; the launch traced here: 29.8 us
  Pallas kernels  19.4 us (64%)
  local copies, waits for them, and re-layouts  9.68 us (32%)
  between operations  0.69 us (2%)
    pallas_call x1, Pallas kernels, shards(): pl.pallas_call(functools.partial(kernel, sizes), out_shape=(block, block,...  19.4 us
    unnamed x24, local copies, waits for them, and re-layouts  9.68 us

profile of v1, /device:TPU:0, one launch (start us, length us, event | category | flops | bytes accessed | tf_op | source)
XLA Modules:
  0.0 29.8 jit_solution(13165485652313502747)
XLA Ops:
  0.6 0.0 copy-start.9
  0.6 0.0 copy-start.8
  0.7 0.0 copy-start.7
  0.7 0.0 copy-start.6
  0.7 0.8 %copy.14.conf = f32[8,3]{1,0:T(8,128)S(1)} copy(f32[8,3]{0,1:T(4,128)} %param.21) | data formatting | bytes 192 | tf_op args[10]
  1.5 0.0 copy-done.9
  1.5 0.0 copy-done.8
  1.5 0.0 copy-done.7
  1.5 0.0 copy-done.6
  1.5 0.0 copy-start
  1.5 1.1 %copy-done = f32[3,16,32,128]{3,2,1,0:T(8,128)S(1)} copy-done((f32[3,16,32,128]{3,2,1,0:T(8,128)S(1)}, f32[3,16,32,128]{3,2,1,0:T(8,128)}, u32[]{:S(2)}) %copy-start) | copy-done | bytes 786456
  2.6 0.0 copy-start.1
  2.6 1.1 %copy-done.1 = f32[3,16,32,128]{3,2,1,0:T(8,128)S(1)} copy-done((f32[3,16,32,128]{3,2,1,0:T(8,128)S(1)}, f32[3,16,32,128]{3,2,1,0:T(8,128)}, u32[]{:S(2)}) %copy-start.1) | copy-done | bytes 786456
  3.7 0.0 copy-start.2
  3.7 1.1 %copy-done.2 = f32[3,16,32,128]{3,2,1,0:T(8,128)S(1)} copy-done((f32[3,16,32,128]{3,2,1,0:T(8,128)S(1)}, f32[3,16,32,128]{3,2,1,0:T(8,128)}, u32[]{:S(2)}) %copy-start.2) | copy-done | bytes 786456
  4.9 0.0 copy-start.3
  4.9 0.9 %copy-done.3 = s32[16,32,128]{2,1,0:T(8,128)S(1)} copy-done((s32[16,32,128]{2,1,0:T(8,128)S(1)}, s32[16,32,128]{2,1,0:T(8,128)}, u32[]{:S(2)}) %copy-start.3) | copy-done | bytes 262168
  5.8 0.0 copy-start.4
  5.8 0.9 %copy-done.4 = s32[16,32,128]{2,1,0:T(8,128)S(1)} copy-done((s32[16,32,128]{2,1,0:T(8,128)S(1)}, s32[16,32,128]{2,1,0:T(8,128)}, u32[]{:S(2)}) %copy-start.4) | copy-done | bytes 262168
  6.8 0.0 copy-start.5
  6.8 0.9 %copy-done.5 = f32[16,32,128]{2,1,0:T(8,128)S(1)} copy-done((f32[16,32,128]{2,1,0:T(8,128)S(1)}, f32[16,32,128]{2,1,0:T(8,128)}, u32[]{:S(2)}) %copy-start.5) | copy-done | bytes 262168
  7.7 19.4 %yee_steps.1 = (f32[3,16,32,128]{3,2,1,0:T(8,128)S(1)}, f32[3,16,32,128]{3,2,1,0:T(8,128)S(1)}, f32[3,16,32,128]{3,2,1,0:T(8,128)S(1)}) custom-call(f32[3]{0:T(128)S(1)} %copy-done.6, f32[3]{0:T(128)S(1)} %copy-done.7, f32[3]{0:T(128)S(1)} %copy-done.8, f32[3]{0:T(128)S(1)} %copy-done.9, f32[8,3]{1,0:T(8,128)S(1)} %copy.14.conf, ...), custom_call_target="tpu_custom_call" | custom-call | flops 20971520 | bytes 5505024 | tf_op jit(solution)/shard_map/yee_steps/pallas_call | solution.py:270
  27.1 0.9 %copy.18 = f32[3,16,32,128]{3,2,1,0:T(8,128)} copy(f32[3,16,32,128]{3,2,1,0:T(8,128)S(1)} %get-tuple-element.6) | data formatting | bytes 1572864
  28.0 0.9 %copy.19 = f32[3,16,32,128]{3,2,1,0:T(8,128)} copy(f32[3,16,32,128]{3,2,1,0:T(8,128)S(1)} %get-tuple-element.7) | data formatting | bytes 1572864
  28.9 0.9 %copy.20 = f32[3,16,32,128]{3,2,1,0:T(8,128)} copy(f32[3,16,32,128]{3,2,1,0:T(8,128)S(1)} %get-tuple-element.8) | data formatting | bytes 1572864
Async XLA Ops:
  0.6 0.8 %copy-start.9 = (f32[3]{0:T(128)S(1)}, f32[3]{0:T(128)}, u32[]{:S(2)}) copy-start(f32[3]{0:T(128)} %relax.1) | copy-start | bytes 40
  0.6 0.8 %copy-start.8 = (f32[3]{0:T(128)S(1)}, f32[3]{0:T(128)}, u32[]{:S(2)}) copy-start(f32[3]{0:T(128)} %deb.1) | copy-start | bytes 40
  0.7 0.8 %copy-start.7 = (f32[3]{0:T(128)S(1)}, f32[3]{0:T(128)}, u32[]{:S(2)}) copy-start(f32[3]{0:T(128)} %cond.1) | copy-start | bytes 40
  0.7 0.8 %copy-start.6 = (f32[3]{0:T(128)S(1)}, f32[3]{0:T(128)}, u32[]{:S(2)}) copy-start(f32[3]{0:T(128)} %perm.1) | copy-start | bytes 40
  1.5 1.1 %copy-start = (f32[3,16,32,128]{3,2,1,0:T(8,128)S(1)}, f32[3,16,32,128]{3,2,1,0:T(8,128)}, u32[]{:S(2)}) copy-start(f32[3,16,32,128]{3,2,1,0:T(8,128)} %e_in.1) | copy-start | bytes 2359300
  2.6 1.1 %copy-start.1 = (f32[3,16,32,128]{3,2,1,0:T(8,128)S(1)}, f32[3,16,32,128]{3,2,1,0:T(8,128)}, u32[]{:S(2)}) copy-start(f32[3,16,32,128]{3,2,1,0:T(8,128)} %h_in.1) | copy-start | bytes 2359300
  3.7 1.1 %copy-start.2 = (f32[3,16,32,128]{3,2,1,0:T(8,128)S(1)}, f32[3,16,32,128]{3,2,1,0:T(8,128)}, u32[]{:S(2)}) copy-start(f32[3,16,32,128]{3,2,1,0:T(8,128)} %p_in.1) | copy-start | bytes 2359300
  4.9 0.9 %copy-start.3 = (s32[16,32,128]{2,1,0:T(8,128)S(1)}, s32[16,32,128]{2,1,0:T(8,128)}, u32[]{:S(2)}) copy-start(s32[16,32,128]{2,1,0:T(8,128)} %m_in.1) | copy-start | bytes 786436
  5.8 0.9 %copy-start.4 = (s32[16,32,128]{2,1,0:T(8,128)S(1)}, s32[16,32,128]{2,1,0:T(8,128)}, u32[]{:S(2)}) copy-start(s32[16,32,128]{2,1,0:T(8,128)} %v_in.1) | copy-start | bytes 786436
  6.8 0.9 %copy-start.5 = (f32[16,32,128]{2,1,0:T(8,128)S(1)}, f32[16,32,128]{2,1,0:T(8,128)}, u32[]{:S(2)}) copy-start(f32[16,32,128]{2,1,0:T(8,128)} %f_in.1) | copy-start | bytes 786436

commit v2 on v1

--- a/solution.py
+++ b/solution.py
@@ -38,15 +38,15 @@
     sizes,
     perm, cond, deb, relax, conf,
     e_in, h_in, p_in, m_in, v_in, f_in,
-    e_out, h_out, p_out,
-    E, H, Q, M, V, F, C, W,
+    E, H, Q,
+    M, V, F, C, W,
     sxe, sxa, sye, sya, sce, sca,
     rxe, rxa, rye, rya, rce, rca,
-    in_sem, out_sem, send_sem, recv_sem,
+    in_sem, send_sem, recv_sem,
 ):
     count_x, count_y = sizes
     nx, ny, nz = m_in.shape
-    mats, vias = perm.shape[0], conf.shape[0]
+    mats, vias = perm.shape[0], conf.shape[1]
     gx, gy = lax.axis_index("gx"), lax.axis_index("gy")
     own = pl.ds(PAD, ny)
     last = nx - 1
@@ -174,7 +174,7 @@
         C[3, x] = bp
         inv = inv * DT
         for comp in range(3):
-            C[4 + comp, x] = inv * pick(rows, [conf[row, comp] for row in range(vias)])
+            C[4 + comp, x] = inv * pick(rows, [conf[comp, row] for row in range(vias)])
         return carry
 
     lax.fori_loop(0, nx, coefficients, 0, unroll=2)
@@ -228,7 +228,7 @@
         E[2, 0, 0:ny] -= C[6, 0] * hy
 
     def advance(t, carry):
-        lax.fori_loop(0, nx, interior, 0, unroll=2)
+        lax.fori_loop(0, nx, interior, 0, unroll=4)
         wait_arrived(t)
         correct(t)
 
@@ -242,10 +242,13 @@
 
     lax.fori_loop(0, STEPS, advance, 0)
 
+
+def write_out(sizes, E, H, Q, e_out, h_out, p_out, sem):
+    nx, ny = sizes
     outs = [
-        pltpu.make_async_copy(E.at[:, 0:nx, 0:ny], e_out, out_sem.at[0]),
-        pltpu.make_async_copy(H.at[:, 1 : nx + 1, PAD : PAD + ny], h_out, out_sem.at[1]),
-        pltpu.make_async_copy(Q, p_out, out_sem.at[2]),
+        pltpu.make_async_copy(E.at[:, 0:nx, 0:ny], e_out, sem.at[0]),
+        pltpu.make_async_copy(H.at[:, 1 : nx + 1, PAD : PAD + ny], h_out, sem.at[1]),
+        pltpu.make_async_copy(Q, p_out, sem.at[2]),
     ]
     for copy in outs:
         copy.start()
@@ -266,16 +269,15 @@
         pltpu.VMEM((STEPS, 8, nz), f32),
     ]
     smem = pl.BlockSpec(memory_space=pltpu.SMEM)
-    hbm = pl.BlockSpec(memory_space=pl.ANY)
-    return pl.pallas_call(
+    hbm = pl.BlockSpec(memory_space=pltpu.HBM)
+    vmem = pl.BlockSpec(memory_space=pltpu.VMEM)
+    padded = pltpu.VMEM((3, nx + 1, ny + PAD, nz), f32)
+    state = pl.pallas_call(
         functools.partial(kernel, sizes),
-        out_shape=(block, block, block),
+        out_shape=(padded, padded, pltpu.VMEM(efield.shape, f32)),
         in_specs=[smem] * 5 + [hbm] * 6,
-        out_specs=(hbm, hbm, hbm),
+        out_specs=(vmem, vmem, vmem),
         scratch_shapes=[
-            pltpu.VMEM((3, nx + 1, ny + PAD, nz), f32),
-            pltpu.VMEM((3, nx + 1, ny + PAD, nz), f32),
-            pltpu.VMEM((3, nx, ny, nz), f32),
             pltpu.VMEM((nx, ny, nz), jnp.int32),
             pltpu.VMEM((nx, ny, nz), jnp.int32),
             pltpu.VMEM((nx, ny, nz), f32),
@@ -286,18 +288,25 @@
         + planes
         + [
             pltpu.SemaphoreType.DMA((6,)),
-            pltpu.SemaphoreType.DMA((3,)),
             pltpu.SemaphoreType.DMA((6, STEPS)),
             pltpu.SemaphoreType.DMA((6, STEPS)),
         ],
         compiler_params=pltpu.CompilerParams(
-            collective_id=0, has_side_effects=True, vmem_limit_bytes=32 * 1024 * 1024
+            collective_id=0, has_side_effects=True, vmem_limit_bytes=56 * 1024 * 1024
         ),
         cost_estimate=pl.CostEstimate(
             flops=80 * STEPS * nx * ny * nz, bytes_accessed=21 * 4 * nx * ny * nz, transcendentals=0
         ),
         name="yee_steps",
-    )(perm, cond, deb, relax, conf, efield, hfield, polar, material_map, via_index, fill)
+    )(perm, cond, deb, relax, conf.T, efield, hfield, polar, material_map, via_index, fill)
+    return pl.pallas_call(
+        functools.partial(write_out, (nx, ny)),
+        out_shape=(block, block, block),
+        in_specs=[pl.BlockSpec(memory_space=pl.ANY)] * 3,
+        out_specs=(hbm, hbm, hbm),
+        scratch_shapes=[pltpu.SemaphoreType.DMA((3,))],
+        name="write_out",
+    )(*state)
 
 
 def solution(mesh):

time: 30.1 us -> 95.6 us (3.18)
  the two profiles are of different devices: /device:TPU:0 before, /device:TPU:9 now
where the time goes in v2:
time: 95.6 us; the launch traced here: 94.7 us
  Pallas kernels  91.2 us (95%)
  local copies, waits for them, and re-layouts  2.87 us (3%)
    pallas_call x1, Pallas kernels, shards(): pl.pallas_call(functools.partial(write_out, (nx, ny)), out_shape=(block,...  72.6 us
    pallas_call x1, Pallas kernels, shards(): pl.pallas_call(functools.partial(kernel, sizes), out_shape=(padded, padde...  18.6 us
    unnamed x6, local copies, waits for them, and re-layouts  2.87 us

profile of v2, /device:TPU:9, one launch (start us, length us, event | category | flops | bytes accessed | tf_op | source)
XLA Modules:
  0.0 94.7 jit_solution(13863747744987864836)
XLA Ops:
  0.6 18.6 %yee_steps.1 = (f32[3,17,40,128]{3,2,1,0:T(8,128)S(1)}, f32[3,17,40,128]{3,2,1,0:T(8,128)S(1)}, f32[3,16,32,128]{3,2,1,0:T(8,128)S(1)}) custom-call(f32[3]{0:T(128)} %perm.1, f32[3]{0:T(128)} %cond.1, f32[3]{0:T(128)} %deb.1, f32[3]{0:T(128)} %relax.1, f32[3,8]{1,0:T(4,128)} %bitcast.1, f32[3,16,32,128]{3,2,1,0:T(8,128)} %e_in.1, f32[3,16,32,128]{3,2,1,0:T(8,128)} %h_in.1, ...), custom_call_target="tpu_custom_call" | custom-call | flops 20971520 | bytes 5505024 | tf_op jit(solution)/shard_map/yee_steps/pallas_call | solution.py:275
  19.2 0.0 copy-start
  19.3 1.0 %copy-done = f32[3,17,40,128]{3,2,1,0:T(8,128)} copy-done((f32[3,17,40,128]{3,2,1,0:T(8,128)}, f32[3,17,40,128]{3,2,1,0:T(8,128)S(1)}, u32[]{:S(2)}) %copy-start) | copy-done | bytes 1044504
  20.2 0.0 copy-start.1
  20.2 1.0 %copy-done.1 = f32[3,17,40,128]{3,2,1,0:T(8,128)} copy-done((f32[3,17,40,128]{3,2,1,0:T(8,128)}, f32[3,17,40,128]{3,2,1,0:T(8,128)S(1)}, u32[]{:S(2)}) %copy-start.1) | copy-done | bytes 1044504
  21.2 0.0 copy-start.2
  21.2 0.9 copy-done.2
  22.1 72.6 %write_out.1 = (f32[3,16,32,128]{3,2,1,0:T(8,128)}, f32[3,16,32,128]{3,2,1,0:T(8,128)}, f32[3,16,32,128]{3,2,1,0:T(8,128)}) custom-call(f32[3,17,40,128]{3,2,1,0:T(8,128)} %copy-done, f32[3,17,40,128]{3,2,1,0:T(8,128)} %copy-done.1, f32[3,16,32,128]{3,2,1,0:T(8,128)} %copy-done.2), custom_call_target="tpu_custom_call" | custom-call | tf_op jit(solution)/shard_map/write_out/pallas_call | solution.py:302
Async XLA Ops:
  19.2 1.0 %copy-start = (f32[3,17,40,128]{3,2,1,0:T(8,128)}, f32[3,17,40,128]{3,2,1,0:T(8,128)S(1)}, u32[]{:S(2)}) copy-start(f32[3,17,40,128]{3,2,1,0:T(8,128)S(1)} %get-tuple-element.6.E) | copy-start | bytes 3133444
  20.2 1.0 %copy-start.1 = (f32[3,17,40,128]{3,2,1,0:T(8,128)}, f32[3,17,40,128]{3,2,1,0:T(8,128)S(1)}, u32[]{:S(2)}) copy-start(f32[3,17,40,128]{3,2,1,0:T(8,128)S(1)} %get-tuple-element.7.H) | copy-start | bytes 3133444
  21.2 0.9 copy-start.2

commit v3 on v2

--- a/solution.py
+++ b/solution.py
@@ -52,6 +52,13 @@
     last = nx - 1
     end = PAD + ny - 1
 
+    height = ny + PAD
+    flat_e = E.reshape(3 * (nx + 1) * height, nz)
+    flat_h = H.reshape(3 * (nx + 1) * height, nz)
+
+    def line(comp, x, row):
+        return pl.ds((comp * (nx + 1) + x) * height + row, nx, stride=height)
+
     def loads():
         return [
             pltpu.make_async_copy(e_in, E.at[:, 0:nx, 0:ny], in_sem.at[0]),
@@ -130,12 +137,12 @@
         sxa[t, 1] = H[2, nx, own] + DT * (E[1, last, 0:ny] + E[0, last, 1 : ny + 1] - ex)
         sce[t] = E[0, last, 0:8]
         sca[t] = E[1, 0, ny - 8 : ny]
-        sye[t, 0] = E[0, 0:nx, 0, :]
-        sye[t, 1] = E[2, 0:nx, 0, :]
-        ey = E[1, 0:nx, ny - 1, :]
-        sya[t, 0] = H[0, 1 : nx + 1, end, :] + DT * (E[2, 0:nx, ny - 1, :] + z_next(ey) - ey)
-        sya[t, 1] = H[2, 1 : nx + 1, end, :] - DT * (
-            E[1, 1 : nx + 1, ny - 1, :] - ey + E[0, 0:nx, ny - 1, :]
+        sye[t, 0] = flat_e[line(0, 0, 0), :]
+        sye[t, 1] = flat_e[line(2, 0, 0), :]
+        ey = flat_e[line(1, 0, ny - 1), :]
+        sya[t, 0] = flat_h[line(0, 1, end), :] + DT * (flat_e[line(2, 0, ny - 1), :] + z_next(ey) - ey)
+        sya[t, 1] = flat_h[line(2, 1, end), :] - DT * (
+            flat_e[line(1, 1, ny - 1), :] - ey + flat_e[line(0, 0, ny - 1), :]
         )
 
     copies = loads()
@@ -177,7 +184,7 @@
             C[4 + comp, x] = inv * pick(rows, [conf[comp, row] for row in range(vias)])
         return carry
 
-    lax.fori_loop(0, nx, coefficients, 0, unroll=2)
+    lax.fori_loop(0, nx, coefficients, 0, unroll=4)
     for comp in range(3):
         W[comp, 0] = C[4 + comp, :, 0, :]
         W[comp, 1] = C[4 + comp, :, ny - 1, :]
@@ -186,36 +193,39 @@
     flag_x = jnp.where(low_x, 1.0, 0.0)
     flag_y = jnp.where(low_y, 1.0, 0.0)
 
-    def interior(x, carry):
+    def update_h(x, carry):
         ex, ey, ez = E[0, x, 0:ny], E[1, x, 0:ny], E[2, x, 0:ny]
         ex_y, ez_y = E[0, x, 1 : ny + 1], E[2, x, 1 : ny + 1]
         ey_x, ez_x = E[1, x + 1, 0:ny], E[2, x + 1, 0:ny]
-        hx = H[0, x + 1, own] - DT * ((ez_y - ez) - (z_next(ey) - ey))
-        hy = H[1, x + 1, own] - DT * ((z_next(ex) - ex) - (ez_x - ez))
-        hz = H[2, x + 1, own] - DT * ((ey_x - ey) - (ex_y - ex))
-        H[0, x + 1, own], H[1, x + 1, own], H[2, x + 1, own] = hx, hy, hz
+        H[0, x + 1, own] = H[0, x + 1, own] - DT * ((ez_y - ez) - (z_next(ey) - ey))
+        H[1, x + 1, own] = H[1, x + 1, own] - DT * ((z_next(ex) - ex) - (ez_x - ez))
+        H[2, x + 1, own] = H[2, x + 1, own] - DT * ((ey_x - ey) - (ex_y - ex))
+        return carry
+
+    def update_e(x, carry):
+        hx, hy, hz = H[0, x + 1, own], H[1, x + 1, own], H[2, x + 1, own]
         below = pl.ds(PAD - 1, ny)
         cx = (hz - H[2, x + 1, below]) - (hy - z_prev(hy))
         cy = (hx - z_prev(hx)) - (hz - H[2, x, own])
         cz = (hy - H[1, x, own]) - (hx - H[0, x + 1, below])
         c1, c2, kp, bp = C[0, x], C[1, x], C[2, x], C[3, x]
-        for comp, (value, curl) in enumerate(((ex, cx), (ey, cy), (ez, cz))):
-            pol = Q[comp, x]
+        for comp, curl in enumerate((cx, cy, cz)):
+            value, pol = E[comp, x, 0:ny], Q[comp, x]
             E[comp, x, 0:ny] = c1 * value + c2 * pol + C[4 + comp, x] * curl
             Q[comp, x] = kp * pol + bp * value
         return carry
 
     def correct(t):
         dhx, dhz = -DT * rye[t, 1], DT * rye[t, 0]
-        H[0, 1 : nx + 1, end, :] += dhx
-        H[2, 1 : nx + 1, end, :] += dhz
-        E[0, 0:nx, ny - 1, :] += W[0, 1] * dhz
-        E[1, 0:nx, ny - 1, :] += W[1, 1] * ((dhx - z_prev(dhx)) - (dhz - row_prev(dhz)))
-        E[2, 0:nx, ny - 1, :] -= W[2, 1] * dhx
+        flat_h[line(0, 1, end), :] += dhx
+        flat_h[line(2, 1, end), :] += dhz
+        flat_e[line(0, 0, ny - 1), :] += W[0, 1] * dhz
+        flat_e[line(1, 0, ny - 1), :] += W[1, 1] * ((dhx - z_prev(dhx)) - (dhz - row_prev(dhz)))
+        flat_e[line(2, 0, ny - 1), :] -= W[2, 1] * dhx
         hx = flag_y * (rya[t, 0] - DT * sye[t, 1])
         hz = flag_y * (rya[t, 1] + DT * (sye[t, 0] - at_row(rca[t, 7:8], last, dhx)))
-        E[0, 0:nx, 0, :] -= W[0, 0] * hz
-        E[2, 0:nx, 0, :] += W[2, 0] * hx
+        flat_e[line(0, 0, 0), :] -= W[0, 0] * hz
+        flat_e[line(2, 0, 0), :] += W[2, 0] * hx
         dhy, dhz = DT * rxe[t, 1], -DT * rxe[t, 0]
         H[1, nx, own] += dhy
         H[2, nx, own] += dhz
@@ -228,7 +238,8 @@
         E[2, 0, 0:ny] -= C[6, 0] * hy
 
     def advance(t, carry):
-        lax.fori_loop(0, nx, interior, 0, unroll=4)
+        lax.fori_loop(0, nx, update_h, 0, unroll=nx)
+        lax.fori_loop(0, nx, update_e, 0, unroll=nx)
         wait_arrived(t)
         correct(t)
 
@@ -305,6 +316,7 @@
         in_specs=[pl.BlockSpec(memory_space=pl.ANY)] * 3,
         out_specs=(hbm, hbm, hbm),
         scratch_shapes=[pltpu.SemaphoreType.DMA((3,))],
+        compiler_params=pltpu.CompilerParams(vmem_limit_bytes=4 * 1024 * 1024),
         name="write_out",
     )(*state)
 

time: 95.6 us -> 21.5 us (0.22)
  the two profiles are of different devices: /device:TPU:9 before, /device:TPU:0 now
where the time goes in v3:
time: 21.5 us; the launch traced here: 21.3 us
  Pallas kernels  20.7 us (96%)
  between operations  0.64 us (3%)
    pallas_call x1, Pallas kernels, shards(): pl.pallas_call(functools.partial(kernel, sizes), out_shape=(padded, padde...  19.3 us
    pallas_call x1, Pallas kernels, shards(): pl.pallas_call(functools.partial(write_out, (nx, ny)), out_shape=(block,...  1.43 us

profile of v3, /device:TPU:0, one launch (start us, length us, event | category | flops | bytes accessed | tf_op | source)
XLA Modules:
  0.0 21.3 jit_solution(10850286619316944149)
XLA Ops:
  0.6 19.3 %yee_steps.1 = (f32[3,17,40,128]{3,2,1,0:T(8,128)S(1)}, f32[3,17,40,128]{3,2,1,0:T(8,128)S(1)}, f32[3,16,32,128]{3,2,1,0:T(8,128)S(1)}) custom-call(f32[3]{0:T(128)} %perm.1, f32[3]{0:T(128)} %cond.1, f32[3]{0:T(128)} %deb.1, f32[3]{0:T(128)} %relax.1, f32[3,8]{1,0:T(4,128)} %bitcast.1, f32[3,16,32,128]{3,2,1,0:T(8,128)} %e_in.1, f32[3,16,32,128]{3,2,1,0:T(8,128)} %h_in.1, ...), custom_call_target="tpu_custom_call" | custom-call | flops 20971520 | bytes 5505024 | tf_op jit(solution)/shard_map/yee_steps/pallas_call | solution.py:286
  19.9 1.4 %write_out.1 = (f32[3,16,32,128]{3,2,1,0:T(8,128)}, f32[3,16,32,128]{3,2,1,0:T(8,128)}, f32[3,16,32,128]{3,2,1,0:T(8,128)}) custom-call(f32[3,17,40,128]{3,2,1,0:T(8,128)S(1)} %get-tuple-element.6.E, f32[3,17,40,128]{3,2,1,0:T(8,128)S(1)} %get-tuple-element.7.H, f32[3,16,32,128]{3,2,1,0:T(8,128)S(1)} %get-tuple-element.8.Q), custom_call_target="tpu_custom_call" | custom-call | tf_op jit(solution)/shard_map/write_out/pallas_call | solution.py:313

commit v4 on v3

--- a/solution.py
+++ b/solution.py
@@ -36,10 +36,11 @@
 
 def kernel(
     sizes,
-    perm, cond, deb, relax, conf,
+    perm_in, cond_in, deb_in, relax_in, conf_in,
     e_in, h_in, p_in, m_in, v_in, f_in,
     E, H, Q,
     M, V, F, C, W,
+    perm, cond, deb, relax, conf,
     sxe, sxa, sye, sya, sce, sca,
     rxe, rxa, rye, rya, rce, rca,
     in_sem, send_sem, recv_sem,
@@ -67,6 +68,11 @@
             pltpu.make_async_copy(v_in, V, in_sem.at[3]),
             pltpu.make_async_copy(f_in, F, in_sem.at[4]),
             pltpu.make_async_copy(p_in, Q, in_sem.at[5]),
+            pltpu.make_async_copy(perm_in, perm, in_sem.at[6]),
+            pltpu.make_async_copy(cond_in, cond, in_sem.at[7]),
+            pltpu.make_async_copy(deb_in, deb, in_sem.at[8]),
+            pltpu.make_async_copy(relax_in, relax, in_sem.at[9]),
+            pltpu.make_async_copy(conf_in, conf, in_sem.at[10]),
         ]
 
     low_x, high_x = gx > 0, gx < count_x - 1
@@ -100,23 +106,20 @@
             device_id_type=MESH,
         )
 
-    def send(t):
-        for k in range(len(routes)):
-            @pl.when(routes[k][1])
+    def each(chosen, which, act):
+        for k in chosen:
+            @pl.when(routes[k][which])
             def _(k=k):
-                remote(k, t).start()
+                act(k)
+
+    def send(t, chosen):
+        each(chosen, 1, lambda k: remote(k, t).start())
 
     def wait_sent(t):
-        for k in range(len(routes)):
-            @pl.when(routes[k][1])
-            def _(k=k):
-                remote(k, t).wait_send()
-
-    def wait_arrived(t):
-        for k in range(len(routes)):
-            @pl.when(routes[k][4])
-            def _(k=k):
-                remote(k, t).wait_recv()
+        each(range(6), 1, lambda k: remote(k, t).wait_send())
+
+    def wait_arrived(t, chosen):
+        each(chosen, 4, lambda k: remote(k, t).wait_recv())
 
     for _, _, _, dest, sender in routes:
         @pl.when(jnp.logical_not(sender))
@@ -130,13 +133,15 @@
             E[comp, x, ny : ny + PAD] = jnp.zeros((PAD, nz), jnp.float32)
             H[comp, x + 1, 0:PAD] = jnp.zeros((PAD, nz), jnp.float32)
 
-    def stage(t):
+    def stage_x(t):
+        sce[t] = E[0, last, 0:8]
+        sca[t] = E[1, 0, ny - 8 : ny]
         sxe[t] = E[1:3, 0, 0:ny]
         ex = E[0, last, 0:ny]
         sxa[t, 0] = H[1, nx, own] - DT * (z_next(ex) - ex + E[2, last, 0:ny])
         sxa[t, 1] = H[2, nx, own] + DT * (E[1, last, 0:ny] + E[0, last, 1 : ny + 1] - ex)
-        sce[t] = E[0, last, 0:8]
-        sca[t] = E[1, 0, ny - 8 : ny]
+
+    def stage_y(t):
         sye[t, 0] = flat_e[line(0, 0, 0), :]
         sye[t, 1] = flat_e[line(2, 0, 0), :]
         ey = flat_e[line(1, 0, ny - 1), :]
@@ -145,14 +150,19 @@
             flat_e[line(1, 1, ny - 1), :] - ey + flat_e[line(0, 0, ny - 1), :]
         )
 
+    def stage_and_send(t):
+        stage_x(t)
+        send(t, (4, 5, 0, 1))
+        stage_y(t)
+        send(t, (2, 3))
+
     copies = loads()
     copies[0].wait()
     copies[1].wait()
-    stage(0)
     pl.semaphore_wait(barrier, sum(jnp.where(route[1], 1, 0) for route in routes))
-    send(0)
-
-    for copy in copies[2:5]:
+    stage_and_send(0)
+
+    for copy in copies[2:5] + copies[6:]:
         copy.wait()
     shape = (ny, nz)
     mat_eps = [jnp.full(shape, perm[m], jnp.float32) for m in range(mats)]
@@ -215,7 +225,7 @@
             Q[comp, x] = kp * pol + bp * value
         return carry
 
-    def correct(t):
+    def correct_y(t):
         dhx, dhz = -DT * rye[t, 1], DT * rye[t, 0]
         flat_h[line(0, 1, end), :] += dhx
         flat_h[line(2, 1, end), :] += dhz
@@ -223,30 +233,36 @@
         flat_e[line(1, 0, ny - 1), :] += W[1, 1] * ((dhx - z_prev(dhx)) - (dhz - row_prev(dhz)))
         flat_e[line(2, 0, ny - 1), :] -= W[2, 1] * dhx
         hx = flag_y * (rya[t, 0] - DT * sye[t, 1])
-        hz = flag_y * (rya[t, 1] + DT * (sye[t, 0] - at_row(rca[t, 7:8], last, dhx)))
+        hz = flag_y * (rya[t, 1] + DT * sye[t, 0])
         flat_e[line(0, 0, 0), :] -= W[0, 0] * hz
         flat_e[line(2, 0, 0), :] += W[2, 0] * hx
+
+    def correct_x(t):
         dhy, dhz = DT * rxe[t, 1], -DT * rxe[t, 0]
-        H[1, nx, own] += dhy
-        H[2, nx, own] += dhz
-        E[0, last, 0:ny] += C[4, last] * ((dhz - row_prev(dhz)) - (dhy - z_prev(dhy)))
+        corner = at_row(DT * rca[t, 7:8], 0, dhy)
+        E[0, last, 0:ny] += C[4, last] * (
+            (dhz - row_prev(dhz)) - (dhy - z_prev(dhy)) + corner
+        )
         E[1, last, 0:ny] -= C[5, last] * dhz
         E[2, last, 0:ny] += C[6, last] * dhy
         hy = flag_x * (rxa[t, 0] + DT * sxe[t, 1])
         hz = flag_x * (rxa[t, 1] - DT * (sxe[t, 0] - at_row(rce[t, 0:1], ny - 1, dhy)))
         E[1, 0, 0:ny] += C[5, 0] * hz
         E[2, 0, 0:ny] -= C[6, 0] * hy
+        H[1, nx, own] += dhy
+        H[2, nx, own] += dhz
 
     def advance(t, carry):
         lax.fori_loop(0, nx, update_h, 0, unroll=nx)
         lax.fori_loop(0, nx, update_e, 0, unroll=nx)
-        wait_arrived(t)
-        correct(t)
+        wait_arrived(t, (2, 3))
+        correct_y(t)
+        wait_arrived(t, (4, 5, 0, 1))
+        correct_x(t)
 
         @pl.when(t < STEPS - 1)
         def _():
-            stage(t + 1)
-            send(t + 1)
+            stage_and_send(t + 1)
 
         wait_sent(t)
         return carry
@@ -279,14 +295,13 @@
         pltpu.VMEM((STEPS, 8, nz), f32),
         pltpu.VMEM((STEPS, 8, nz), f32),
     ]
-    smem = pl.BlockSpec(memory_space=pltpu.SMEM)
     hbm = pl.BlockSpec(memory_space=pltpu.HBM)
     vmem = pl.BlockSpec(memory_space=pltpu.VMEM)
     padded = pltpu.VMEM((3, nx + 1, ny + PAD, nz), f32)
     state = pl.pallas_call(
         functools.partial(kernel, sizes),
         out_shape=(padded, padded, pltpu.VMEM(efield.shape, f32)),
-        in_specs=[smem] * 5 + [hbm] * 6,
+        in_specs=[hbm] * 11,
         out_specs=(vmem, vmem, vmem),
         scratch_shapes=[
             pltpu.VMEM((nx, ny, nz), jnp.int32),
@@ -295,10 +310,11 @@
             pltpu.VMEM((7, nx, ny, nz), f32),
             pltpu.VMEM((3, 2, nx, nz), f32),
         ]
+        + [pltpu.SMEM(table.shape, f32) for table in (perm, cond, deb, relax, conf.T)]
         + planes
         + planes
         + [
-            pltpu.SemaphoreType.DMA((6,)),
+            pltpu.SemaphoreType.DMA((11,)),
             pltpu.SemaphoreType.DMA((6, STEPS)),
             pltpu.SemaphoreType.DMA((6, STEPS)),
         ],

time: 21.5 us -> 20.7 us (0.963)
  Pallas kernels: 20.7 us -> 19.9 us
    pallas_call x1, Pallas kernels: 19.3 us -> 18.5 us  [shards(): pl.pallas_call(functools.partial(kernel, sizes), out_shape=(padded, padde...]
where the time goes in v4:
time: 20.7 us; the launch traced here: 20.6 us
  Pallas kernels  19.9 us (96%)
  between operations  0.64 us (3%)
    pallas_call x1, Pallas kernels, shards(): pl.pallas_call(functools.partial(kernel, sizes), out_shape=(padded, padde...  18.5 us
    pallas_call x1, Pallas kernels, shards(): pl.pallas_call(functools.partial(write_out, (nx, ny)), out_shape=(block,...  1.43 us

profile of v4, /device:TPU:0, one launch (start us, length us, event | category | flops | bytes accessed | tf_op | source)
XLA Modules:
  0.0 20.6 jit_solution(16051564004348557064)
XLA Ops:
  0.6 18.5 %yee_steps.1 = (f32[3,17,40,128]{3,2,1,0:T(8,128)S(1)}, f32[3,17,40,128]{3,2,1,0:T(8,128)S(1)}, f32[3,16,32,128]{3,2,1,0:T(8,128)S(1)}) custom-call(f32[3]{0:T(128)} %perm_in.1, f32[3]{0:T(128)} %cond_in.1, f32[3]{0:T(128)} %deb_in.1, f32[3]{0:T(128)} %relax_in.1, f32[3,8]{1,0:T(4,128)} %bitcast.1, f32[3,16,32,128]{3,2,1,0:T(8,128)} %e_in.1, ...), custom_call_target="tpu_custom_call" | custom-call | flops 20971520 | bytes 5505024 | tf_op jit(solution)/shard_map/yee_steps/pallas_call | solution.py:301
  19.2 1.4 %write_out.1 = (f32[3,16,32,128]{3,2,1,0:T(8,128)}, f32[3,16,32,128]{3,2,1,0:T(8,128)}, f32[3,16,32,128]{3,2,1,0:T(8,128)}) custom-call(f32[3,17,40,128]{3,2,1,0:T(8,128)S(1)} %get-tuple-element.6.E, f32[3,17,40,128]{3,2,1,0:T(8,128)S(1)} %get-tuple-element.7.H, f32[3,16,32,128]{3,2,1,0:T(8,128)S(1)} %get-tuple-element.8.Q), custom_call_target="tpu_custom_call" | custom-call | tf_op jit(solution)/shard_map/write_out/pallas_call | solution.py:329

commit v5 on v4

--- a/solution.py
+++ b/solution.py
@@ -11,6 +11,11 @@
 DT = 0.55
 PAD = 8
 MESH = pl.DeviceIdType.MESH
+
+
+def halves(count):
+    half = (count + 1) // 2
+    return [(0, half), (half, count - half)] if count > 1 else [(0, count)]
 
 
 def z_next(value):
@@ -61,19 +66,20 @@
         return pl.ds((comp * (nx + 1) + x) * height + row, nx, stride=height)
 
     def loads():
-        return [
-            pltpu.make_async_copy(e_in, E.at[:, 0:nx, 0:ny], in_sem.at[0]),
-            pltpu.make_async_copy(h_in, H.at[:, 1 : nx + 1, PAD : PAD + ny], in_sem.at[1]),
-            pltpu.make_async_copy(m_in, M, in_sem.at[2]),
-            pltpu.make_async_copy(v_in, V, in_sem.at[3]),
-            pltpu.make_async_copy(f_in, F, in_sem.at[4]),
-            pltpu.make_async_copy(p_in, Q, in_sem.at[5]),
-            pltpu.make_async_copy(perm_in, perm, in_sem.at[6]),
-            pltpu.make_async_copy(cond_in, cond, in_sem.at[7]),
-            pltpu.make_async_copy(deb_in, deb, in_sem.at[8]),
-            pltpu.make_async_copy(relax_in, relax, in_sem.at[9]),
-            pltpu.make_async_copy(conf_in, conf, in_sem.at[10]),
-        ]
+        fields = []
+        for comp in range(3):
+            for x, wide in halves(nx):
+                part = (comp, pl.ds(x, wide))
+                fields.append((e_in.at[part], E.at[comp, pl.ds(x, wide), pl.ds(0, ny)]))
+                fields.append((h_in.at[part], H.at[comp, pl.ds(x + 1, wide), own]))
+        tables = [(perm_in, perm), (cond_in, cond), (deb_in, deb), (relax_in, relax), (conf_in, conf)]
+        cells = [(m_in, M), (v_in, V), (f_in, F)]
+        pols = [(p_in.at[comp], Q.at[comp]) for comp in range(3)]
+        pairs = fields + tables + cells + pols
+        copies = [pltpu.make_async_copy(a, b, in_sem.at[k]) for k, (a, b) in enumerate(pairs)]
+        cut = len(fields)
+        end_cells = cut + len(tables) + len(cells)
+        return copies[:cut], copies[cut:end_cells], copies[end_cells:]
 
     low_x, high_x = gx > 0, gx < count_x - 1
     low_y, high_y = gy > 0, gy < count_y - 1
@@ -92,7 +98,8 @@
         def _(target=target):
             pl.semaphore_signal(barrier, inc=1, device_id=target, device_id_type=MESH)
 
-    for copy in loads():
+    first, second, third = loads()
+    for copy in first + second + third:
         copy.start()
 
     def remote(k, t):
@@ -133,10 +140,12 @@
             E[comp, x, ny : ny + PAD] = jnp.zeros((PAD, nz), jnp.float32)
             H[comp, x + 1, 0:PAD] = jnp.zeros((PAD, nz), jnp.float32)
 
-    def stage_x(t):
-        sce[t] = E[0, last, 0:8]
+    def stage_first(t):
         sca[t] = E[1, 0, ny - 8 : ny]
         sxe[t] = E[1:3, 0, 0:ny]
+
+    def stage_last(t):
+        sce[t] = E[0, last, 0:8]
         ex = E[0, last, 0:ny]
         sxa[t, 0] = H[1, nx, own] - DT * (z_next(ex) - ex + E[2, last, 0:ny])
         sxa[t, 1] = H[2, nx, own] + DT * (E[1, last, 0:ny] + E[0, last, 1 : ny + 1] - ex)
@@ -150,19 +159,17 @@
             flat_e[line(1, 1, ny - 1), :] - ey + flat_e[line(0, 0, ny - 1), :]
         )
 
-    def stage_and_send(t):
-        stage_x(t)
-        send(t, (4, 5, 0, 1))
-        stage_y(t)
-        send(t, (2, 3))
-
-    copies = loads()
-    copies[0].wait()
-    copies[1].wait()
+    for copy in first:
+        copy.wait()
     pl.semaphore_wait(barrier, sum(jnp.where(route[1], 1, 0) for route in routes))
-    stage_and_send(0)
-
-    for copy in copies[2:5] + copies[6:]:
+    stage_first(0)
+    send(0, (5, 0))
+    stage_last(0)
+    send(0, (4, 1))
+    stage_y(0)
+    send(0, (2, 3))
+
+    for copy in second:
         copy.wait()
     shape = (ny, nz)
     mat_eps = [jnp.full(shape, perm[m], jnp.float32) for m in range(mats)]
@@ -198,7 +205,8 @@
     for comp in range(3):
         W[comp, 0] = C[4 + comp, :, 0, :]
         W[comp, 1] = C[4 + comp, :, ny - 1, :]
-    copies[5].wait()
+    for copy in third:
+        copy.wait()
 
     flag_x = jnp.where(low_x, 1.0, 0.0)
     flag_y = jnp.where(low_y, 1.0, 0.0)
@@ -237,7 +245,14 @@
         flat_e[line(0, 0, 0), :] -= W[0, 0] * hz
         flat_e[line(2, 0, 0), :] += W[2, 0] * hx
 
-    def correct_x(t):
+    def correct_first(t):
+        corner = at_row(rce[t, 0:1], ny - 1, rxa[t, 0])
+        hy = flag_x * (rxa[t, 0] + DT * sxe[t, 1])
+        hz = flag_x * (rxa[t, 1] - DT * (sxe[t, 0] - corner))
+        E[1, 0, 0:ny] += C[5, 0] * hz
+        E[2, 0, 0:ny] -= C[6, 0] * hy
+
+    def correct_last(t):
         dhy, dhz = DT * rxe[t, 1], -DT * rxe[t, 0]
         corner = at_row(DT * rca[t, 7:8], 0, dhy)
         E[0, last, 0:ny] += C[4, last] * (
@@ -245,24 +260,32 @@
         )
         E[1, last, 0:ny] -= C[5, last] * dhz
         E[2, last, 0:ny] += C[6, last] * dhy
-        hy = flag_x * (rxa[t, 0] + DT * sxe[t, 1])
-        hz = flag_x * (rxa[t, 1] - DT * (sxe[t, 0] - at_row(rce[t, 0:1], ny - 1, dhy)))
-        E[1, 0, 0:ny] += C[5, 0] * hz
-        E[2, 0, 0:ny] -= C[6, 0] * hy
         H[1, nx, own] += dhy
         H[2, nx, own] += dhz
 
     def advance(t, carry):
         lax.fori_loop(0, nx, update_h, 0, unroll=nx)
         lax.fori_loop(0, nx, update_e, 0, unroll=nx)
+        more = t < STEPS - 1
         wait_arrived(t, (2, 3))
         correct_y(t)
-        wait_arrived(t, (4, 5, 0, 1))
-        correct_x(t)
-
-        @pl.when(t < STEPS - 1)
+        wait_arrived(t, (1, 4))
+        correct_first(t)
+
+        @pl.when(more)
         def _():
-            stage_and_send(t + 1)
+            stage_first(t + 1)
+            send(t + 1, (5, 0))
+
+        wait_arrived(t, (0, 5))
+        correct_last(t)
+
+        @pl.when(more)
+        def _():
+            stage_last(t + 1)
+            send(t + 1, (4, 1))
+            stage_y(t + 1)
+            send(t + 1, (2, 3))
 
         wait_sent(t)
         return carry
@@ -272,14 +295,17 @@
 
 def write_out(sizes, E, H, Q, e_out, h_out, p_out, sem):
     nx, ny = sizes
-    outs = [
-        pltpu.make_async_copy(E.at[:, 0:nx, 0:ny], e_out, sem.at[0]),
-        pltpu.make_async_copy(H.at[:, 1 : nx + 1, PAD : PAD + ny], h_out, sem.at[1]),
-        pltpu.make_async_copy(Q, p_out, sem.at[2]),
-    ]
-    for copy in outs:
+    pairs = []
+    for comp in range(3):
+        for x, wide in halves(nx):
+            part = (comp, pl.ds(x, wide))
+            pairs.append((E.at[comp, pl.ds(x, wide), pl.ds(0, ny)], e_out.at[part]))
+            pairs.append((H.at[comp, pl.ds(x + 1, wide), pl.ds(PAD, ny)], h_out.at[part]))
+            pairs.append((Q.at[part], p_out.at[part]))
+    copies = [pltpu.make_async_copy(a, b, sem.at[k]) for k, (a, b) in enumerate(pairs)]
+    for copy in copies:
         copy.start()
-    for copy in outs:
+    for copy in copies:
         copy.wait()
 
 
@@ -314,7 +340,7 @@
         + planes
         + planes
         + [
-            pltpu.SemaphoreType.DMA((11,)),
+            pltpu.SemaphoreType.DMA((6 * len(halves(nx)) + 11,)),
             pltpu.SemaphoreType.DMA((6, STEPS)),
             pltpu.SemaphoreType.DMA((6, STEPS)),
         ],
@@ -331,7 +357,7 @@
         out_shape=(block, block, block),
         in_specs=[pl.BlockSpec(memory_space=pl.ANY)] * 3,
         out_specs=(hbm, hbm, hbm),
-        scratch_shapes=[pltpu.SemaphoreType.DMA((3,))],
+        scratch_shapes=[pltpu.SemaphoreType.DMA((9 * len(halves(nx)),))],
         compiler_params=pltpu.CompilerParams(vmem_limit_bytes=4 * 1024 * 1024),
         name="write_out",
     )(*state)

time: 20.7 us -> 19.1 us (0.923)
  the two profiles are of different devices: /device:TPU:0 before, /device:TPU:9 now
where the time goes in v5:
time: 19.1 us; the launch traced here: 19 us
  Pallas kernels  18.3 us (96%)
  between operations  0.64 us (3%)
    pallas_call x1, Pallas kernels, shards(): pl.pallas_call(functools.partial(kernel, sizes), out_shape=(padded, padde...  16.8 us
    pallas_call x1, Pallas kernels, shards(): pl.pallas_call(functools.partial(write_out, (nx, ny)), out_shape=(block,...  1.54 us

profile of v5, /device:TPU:9, one launch (start us, length us, event | category | flops | bytes accessed | tf_op | source)
XLA Modules:
  0.0 19.0 jit_solution(8949474605567467174)
XLA Ops:
  0.6 16.8 %yee_steps.1 = (f32[3,17,40,128]{3,2,1,0:T(8,128)S(1)}, f32[3,17,40,128]{3,2,1,0:T(8,128)S(1)}, f32[3,16,32,128]{3,2,1,0:T(8,128)S(1)}) custom-call(f32[3]{0:T(128)} %perm_in.1, f32[3]{0:T(128)} %cond_in.1, f32[3]{0:T(128)} %deb_in.1, f32[3]{0:T(128)} %relax_in.1, f32[3,8]{1,0:T(4,128)} %bitcast.1, f32[3,16,32,128]{3,2,1,0:T(8,128)} %e_in.1, ...), custom_call_target="tpu_custom_call" | custom-call | flops 20971520 | bytes 5505024 | tf_op jit(solution)/shard_map/yee_steps/pallas_call | solution.py:327
  17.4 1.5 %write_out.1 = (f32[3,16,32,128]{3,2,1,0:T(8,128)}, f32[3,16,32,128]{3,2,1,0:T(8,128)}, f32[3,16,32,128]{3,2,1,0:T(8,128)}) custom-call(f32[3,17,40,128]{3,2,1,0:T(8,128)S(1)} %get-tuple-element.6.E, f32[3,17,40,128]{3,2,1,0:T(8,128)S(1)} %get-tuple-element.7.H, f32[3,16,32,128]{3,2,1,0:T(8,128)S(1)} %get-tuple-element.8.Q), custom_call_target="tpu_custom_call" | custom-call | tf_op jit(solution)/shard_map/write_out/pallas_call | solution.py:355

commit v6 on v5

--- a/solution.py
+++ b/solution.py
@@ -99,7 +99,7 @@
             pl.semaphore_signal(barrier, inc=1, device_id=target, device_id_type=MESH)
 
     first, second, third = loads()
-    for copy in first + second + third:
+    for copy in first[0::2] + first[1::2]:
         copy.start()
 
     def remote(k, t):
@@ -159,11 +159,15 @@
             flat_e[line(1, 1, ny - 1), :] - ey + flat_e[line(0, 0, ny - 1), :]
         )
 
-    for copy in first:
-        copy.wait()
+    for copy in first[0::2]:
+        copy.wait()
+    stage_first(0)
     pl.semaphore_wait(barrier, sum(jnp.where(route[1], 1, 0) for route in routes))
-    stage_first(0)
     send(0, (5, 0))
+    for copy in first[1::2]:
+        copy.wait()
+    for copy in second + third:
+        copy.start()
     stage_last(0)
     send(0, (4, 1))
     stage_y(0)

time: 19.1 us -> 19.1 us (level)
  no operation moved by 1% of the time
where the time goes in v6:
time: 19.1 us; the launch traced here: 19 us
  Pallas kernels  18.3 us (96%)
  between operations  0.64 us (3%)
    pallas_call x1, Pallas kernels, shards(): pl.pallas_call(functools.partial(kernel, sizes), out_shape=(padded, padde...  16.8 us
    pallas_call x1, Pallas kernels, shards(): pl.pallas_call(functools.partial(write_out, (nx, ny)), out_shape=(block,...  1.54 us

profile of v6, /device:TPU:9, one launch (start us, length us, event | category | flops | bytes accessed | tf_op | source)
XLA Modules:
  0.0 19.0 jit_solution(15770655233947900554)
XLA Ops:
  0.6 16.8 %yee_steps.1 = (f32[3,17,40,128]{3,2,1,0:T(8,128)S(1)}, f32[3,17,40,128]{3,2,1,0:T(8,128)S(1)}, f32[3,16,32,128]{3,2,1,0:T(8,128)S(1)}) custom-call(f32[3]{0:T(128)} %perm_in.1, f32[3]{0:T(128)} %cond_in.1, f32[3]{0:T(128)} %deb_in.1, f32[3]{0:T(128)} %relax_in.1, f32[3,8]{1,0:T(4,128)} %bitcast.1, f32[3,16,32,128]{3,2,1,0:T(8,128)} %e_in.1, ...), custom_call_target="tpu_custom_call" | custom-call | flops 20971520 | bytes 5505024 | tf_op jit(solution)/shard_map/yee_steps/pallas_call | solution.py:331
  17.4 1.5 %write_out.1 = (f32[3,16,32,128]{3,2,1,0:T(8,128)}, f32[3,16,32,128]{3,2,1,0:T(8,128)}, f32[3,16,32,128]{3,2,1,0:T(8,128)}) custom-call(f32[3,17,40,128]{3,2,1,0:T(8,128)S(1)} %get-tuple-element.6.E, f32[3,17,40,128]{3,2,1,0:T(8,128)S(1)} %get-tuple-element.7.H, f32[3,16,32,128]{3,2,1,0:T(8,128)S(1)} %get-tuple-element.8.Q), custom_call_target="tpu_custom_call" | custom-call | tf_op jit(solution)/shard_map/write_out/pallas_call | solution.py:359

commit v7 on v5

--- a/solution.py
+++ b/solution.py
@@ -264,8 +264,8 @@
         H[2, nx, own] += dhz
 
     def advance(t, carry):
-        lax.fori_loop(0, nx, update_h, 0, unroll=nx)
-        lax.fori_loop(0, nx, update_e, 0, unroll=nx)
+        lax.fori_loop(0, nx, update_h, 0, unroll=4)
+        lax.fori_loop(0, nx, update_e, 0, unroll=4)
         more = t < STEPS - 1
         wait_arrived(t, (2, 3))
         correct_y(t)

time: 19.1 us -> 19.1 us (level)
  no operation moved by 1% of the time
where the time goes in v7:
time: 19.1 us; the launch traced here: 19 us
  Pallas kernels  18.3 us (96%)
  between operations  0.64 us (3%)
    pallas_call x1, Pallas kernels, shards(): pl.pallas_call(functools.partial(kernel, sizes), out_shape=(padded, padde...  16.8 us
    pallas_call x1, Pallas kernels, shards(): pl.pallas_call(functools.partial(write_out, (nx, ny)), out_shape=(block,...  1.54 us

profile of v7, /device:TPU:9, one launch (start us, length us, event | category | flops | bytes accessed | tf_op | source)
XLA Modules:
  0.0 19.0 jit_solution(15324854383201703282)
XLA Ops:
  0.6 16.8 %yee_steps.1 = (f32[3,17,40,128]{3,2,1,0:T(8,128)S(1)}, f32[3,17,40,128]{3,2,1,0:T(8,128)S(1)}, f32[3,16,32,128]{3,2,1,0:T(8,128)S(1)}) custom-call(f32[3]{0:T(128)} %perm_in.1, f32[3]{0:T(128)} %cond_in.1, f32[3]{0:T(128)} %deb_in.1, f32[3]{0:T(128)} %relax_in.1, f32[3,8]{1,0:T(4,128)} %bitcast.1, f32[3,16,32,128]{3,2,1,0:T(8,128)} %e_in.1, ...), custom_call_target="tpu_custom_call" | custom-call | flops 20971520 | bytes 5505024 | tf_op jit(solution)/shard_map/yee_steps/pallas_call | solution.py:327
  17.4 1.5 %write_out.1 = (f32[3,16,32,128]{3,2,1,0:T(8,128)}, f32[3,16,32,128]{3,2,1,0:T(8,128)}, f32[3,16,32,128]{3,2,1,0:T(8,128)}) custom-call(f32[3,17,40,128]{3,2,1,0:T(8,128)S(1)} %get-tuple-element.6.E, f32[3,17,40,128]{3,2,1,0:T(8,128)S(1)} %get-tuple-element.7.H, f32[3,16,32,128]{3,2,1,0:T(8,128)S(1)} %get-tuple-element.8.Q), custom_call_target="tpu_custom_call" | custom-call | tf_op jit(solution)/shard_map/write_out/pallas_call | solution.py:355
